TPU v7x, 32 devices: a whole 2x2x4 slice. The times are simulated.
32 devices in a mesh: grp: 2 (over x), ep: 16 (over z, y, core).
Axes of the slice: x: 2, y: 2, z: 4, core: 2. Of those that a mesh axis runs over, the one named last changes fastest.
Arguments:
- tokens: bfloat16 [4096, 2048], P(('grp', 'ep')), parts along dimension 0, may hold values from -6 to 6
- cotangent: bfloat16 [4096, 2048], P(('grp', 'ep')), parts along dimension 0, may hold values from -6 to 6
- route_ids: int32 [4096, 8], P(('grp', 'ep')), parts along dimension 0, may hold values from 0 to 15, all different within a row; in each aligned block of 128 rows (0 to 127, 128 to 255, ...) at most 96 rows name the same one
- route_weights: float32 [4096, 8], P(('grp', 'ep')), parts along dimension 0, may hold values from 0.05 to 1
- owner: int32 [32], P('grp'), parts along dimension 0, may hold values from 0 to 15, each once
- base_joined: bfloat16 [16, 2048, 768], P('ep'), may hold values from -0.125 to 0.125
- base_down: bfloat16 [16, 384, 2048], P('ep'), may hold values from -0.3125 to 0.3125
- master: float32 [32, 167936], P('grp', 'ep'), parts along dimension 0, may hold values from -0.3 to 0.3
- moment: float32 [32, 167936], P('grp', 'ep'), parts along dimension 0, may hold values from -0.6 to 0.6
- second: float32 [32, 167936], P('grp', 'ep'), parts along dimension 0, may hold values from 0.003 to 0.3
- step_rows: bfloat16 [4, 256, 2048], P(None, ('grp', 'ep')), parts along dimension 1, may hold values from -6 to 6
- step_ids: int32 [4, 256, 8], P(None, ('grp', 'ep')), parts along dimension 1, may hold values from 0 to 15, all different within a row; in each aligned block of 8 rows (0 to 7, 8 to 15, ..., all dimensions but the last counted through in order) at most 6 rows name the same one
- step_weights: float32 [4, 256, 8], P(None, ('grp', 'ep')), parts along dimension 1, may hold values from 0.05 to 1
Outputs:
- updated: float32 [32, 167936], P('grp', 'ep'), parts along dimension 0
- decoded: bfloat16 [4, 256, 2048], P(None, ('grp', 'ep')), parts along dimension 1
There are 2 independent parts, one for each index of `grp`. A program takes and returns all parts, laid end to end along the dimension named above; an argument that names none is the same for every part. Nothing has to cross between parts.
Inputs may be any that keep to these rules, and one draw needn't show every extreme that they name: `route_ids`: each row names 8 different experts; in the rows of one device no expert is named more than 96 times, a bound that some block reaches. `step_ids`: each row names 8 different experts; in the rows of one device in one step no expert is named more than 6 times, a bound that some block reaches. `owner`: A permutation of the devices.
All inputs are finite; a program needn't handle non-finite values.
Results may differ from a plain program's by a relative error of at most 0.012.
The roundings to bfloat16 on the way count: a program that leaves them out, or rounds other values in their place, can miss the bound.
Values may be sent and summed in bfloat16 or wider, within the bound.
A program may use at most 128 MiB of HBM per device.

v0:
```python
import jax
import jax.numpy as jnp
from jax import lax
from jax.experimental import pallas as pl
from jax.experimental.pallas import tpu as pltpu
from jax.sharding import PartitionSpec as P

D = 2048
FF = 384
RANK = 32


adapter_scale_factor = 0.5
learn_rate = 0.05
beta_one = 0.9
beta_two = 0.999
decay_rate = 0.1
epsilon = 1e-08
bias_one = 1.0 - 0.9**50
bias_two = 1.0 - 0.999**50


def product(left, right):
    return jnp.dot(left, right, preferred_element_type=jnp.float32)


def unpack(flat):
    cut_one = D * RANK
    cut_two = cut_one + RANK * 2 * FF
    cut_three = cut_two + FF * RANK
    a_in = flat[:cut_one].reshape(D, RANK)
    b_in = flat[cut_one:cut_two].reshape(RANK, 2 * FF)
    a_out = flat[cut_two:cut_three].reshape(FF, RANK)
    b_out = flat[cut_three:].reshape(RANK, D)
    return (a_in, b_in, a_out, b_out)


def expert_grads(rows, grad_rows, joined_weight, down_weight, flat_bf):
    a_in, b_in, a_out, b_out = unpack(flat_bf)
    mid_in = product(rows, a_in).astype(jnp.bfloat16)
    joined = product(rows, joined_weight) + adapter_scale_factor * product(mid_in, b_in)
    gate = joined[:, :FF]
    up_part = joined[:, FF:]
    sigma = jax.nn.sigmoid(gate)
    active = gate * sigma
    hidden = (active * up_part).astype(jnp.bfloat16)
    mid_out = product(hidden, a_out).astype(jnp.bfloat16)
    grad_b_out = adapter_scale_factor * product(mid_out.T, grad_rows)
    back_mid = (adapter_scale_factor * product(grad_rows, b_out.T)).astype(jnp.bfloat16)
    grad_a_out = product(hidden.T, back_mid)
    back_hidden = product(grad_rows, down_weight.T) + product(back_mid, a_out.T)
    back_gate = back_hidden * up_part * sigma * (1.0 + gate * (1.0 - sigma))
    back_up = back_hidden * active
    back_joined = jnp.concatenate([back_gate, back_up], axis=1).astype(jnp.bfloat16)
    grad_b_in = adapter_scale_factor * product(mid_in.T, back_joined)
    back_in = (adapter_scale_factor * product(back_joined, b_in.T)).astype(jnp.bfloat16)
    grad_a_in = product(rows.T, back_in)
    return jnp.concatenate(
        [
            grad_a_in.reshape(-1),
            grad_b_in.reshape(-1),
            grad_a_out.reshape(-1),
            grad_b_out.reshape(-1),
        ]
    )


def train_kernel(
    tok,
    cot,
    weight,
    wf,
    wd,
    a_in,
    b_in,
    a_out,
    b_out,
    out_a_in,
    out_b_in,
    out_a_out,
    out_b_out,
    held_tok,
    held_cot,
    send,
    recv,
):
    devices = lax.axis_size("ep")
    chips = devices // 2
    half = chips // 2
    me = lax.axis_index("ep")
    core = lax.rem(me, 2)
    chip = me // 2
    place = jnp.where(lax.rem(chip, 2) == 0, chip // 2, chips - 1 - chip // 2)

    def chip_at(position):
        position = lax.rem(position + 2 * chips, chips)
        return jnp.where(position < half, 2 * position, 2 * (chips - 1 - position) + 1)

    right = 2 * chip_at(place + 1) + core
    left = 2 * chip_at(place - 1) + core
    sibling = 2 * chip + 1 - core
    held = (held_tok, held_cot)

    barrier = pltpu.get_barrier_semaphore()
    for other in (left, right, sibling):
        pl.semaphore_signal(
            barrier, inc=1, device_id={"ep": other}, device_id_type=pl.DeviceIdType.MESH
        )
    pl.semaphore_wait(barrier, 3)

    def move(kind, source, slot, other):
        return pltpu.make_async_remote_copy(
            src_ref=source,
            dst_ref=held[kind].at[slot],
            send_sem=send.at[kind, slot],
            recv_sem=recv.at[kind, slot],
            device_id={"ep": other},
            device_id_type=pl.DeviceIdType.MESH,
        )

    for kind, own in ((0, tok), (1, cot)):
        move(kind, own, 2, right).start()
        move(kind, own, 3, left).start()
        move(kind, own, 1, sibling).start()
    held_tok[0] = tok[...]
    held_cot[0] = cot[...]
    for out in (out_a_in, out_b_in, out_a_out, out_b_out):
        out[...] = jnp.zeros_like(out)

    def arrived(kind, slot):
        move(kind, held[kind].at[slot], slot, sibling).wait_recv()

    def outer(left_op, right_op):
        return lax.dot_general(
            left_op, right_op, (((0,), (0,)), ((), ())), preferred_element_type=jnp.float32
        )

    def times_transposed(left_op, right_op):
        return lax.dot_general(
            left_op, right_op, (((1,), (1,)), ((), ())), preferred_element_type=jnp.float32
        )

    def learn(tile, first, second):
        count, width = tok.shape
        pair = pl.ds(2 * tile, 2)
        rows = held_tok[pair].reshape(2 * count, width)
        gain = jnp.concatenate([weight[first], weight[second]], axis=0)
        grad = (gain * held_cot[pair].reshape(2 * count, width).astype(jnp.float32)).astype(
            jnp.bfloat16
        )
        mid_in = product(rows, a_in[...]).astype(jnp.bfloat16)
        joined = product(rows, wf[...]) + adapter_scale_factor * product(mid_in, b_in[...])
        gate = joined[:, :FF]
        up_part = joined[:, FF:]
        sigma = jax.nn.sigmoid(gate)
        active = gate * sigma
        hidden = (active * up_part).astype(jnp.bfloat16)
        mid_out = product(hidden, a_out[...]).astype(jnp.bfloat16)
        out_b_out[...] += adapter_scale_factor * outer(mid_out, grad)
        back_mid = (adapter_scale_factor * times_transposed(grad, b_out[...])).astype(jnp.bfloat16)
        out_a_out[...] += outer(back_mid, hidden)
        back_hidden = times_transposed(grad, wd[...]) + times_transposed(back_mid, a_out[...])
        back_gate = back_hidden * up_part * sigma * (1.0 + gate * (1.0 - sigma))
        back_up = back_hidden * active
        back_joined = jnp.concatenate([back_gate, back_up], axis=1).astype(jnp.bfloat16)
        out_b_in[...] += adapter_scale_factor * outer(mid_in, back_joined)
        back_in = (adapter_scale_factor * times_transposed(back_joined, b_in[...])).astype(
            jnp.bfloat16
        )
        out_a_in[...] += outer(back_in, rows)

    def step(s, carry):
        base = 4 * s - 2

        @pl.when(s == 0)
        def _():
            for kind in (0, 1):
                arrived(kind, 1)

        @pl.when((s > 0) & (s < half))
        def _():
            for kind in (0, 1):
                for way, onward in ((0, right), (1, left)):
                    slot = base + way
                    arrived(kind, slot)

                    @pl.when(s < half - 1)
                    def _():
                        move(kind, held[kind].at[slot], slot + 4, onward).start()

                    if way == kind:

                        @pl.when(s == half - 1)
                        def _():
                            move(kind, held[kind].at[slot], 4 * half - 2, onward).start()

                    move(kind, held[kind].at[slot], slot + 2, sibling).start()
            for kind in (0, 1):
                for way in (0, 1):
                    arrived(kind, base + 2 + way)

        @pl.when(s == half)
        def _():
            for kind in (0, 1):
                arrived(kind, base)
                move(kind, held[kind].at[base], base + 1, sibling).start()
            for kind in (0, 1):
                arrived(kind, base + 1)

        single = (s == 0) | (s == half)
        from_left = 2 * chip_at(place - s)
        from_right = 2 * chip_at(place + s)

        def tile_of(j, inner):
            which = core + j - 2 * core * j
            second = jnp.where(single, from_left + 1 - core, from_right + which)
            learn(jnp.where(s == 0, 0, 2 * s - 1) + j, from_left + which, second)
            return inner

        lax.fori_loop(0, jnp.where(single, 1, 2), tile_of, 0)
        return carry

    lax.fori_loop(0, half + 1, step, 0)

    def sent(slot, carry):
        for kind in (0, 1):
            move(kind, held[kind].at[slot], slot, sibling).wait_send()
        return carry

    lax.fori_loop(1, devices, sent, 0)


def train(tokens, cotangent, weight, joined_weight, down_weight, flat_bf):
    devices = lax.axis_size("ep")
    count, width = tokens.shape
    a_in, b_in, a_out, b_out = unpack(flat_bf)
    shape = lambda *size: jax.ShapeDtypeStruct(size, jnp.float32)
    vmem = pl.BlockSpec(memory_space=pltpu.VMEM)
    g_a_in, g_b_in, g_a_out, g_b_out = pl.pallas_call(
        train_kernel,
        out_shape=(shape(RANK, width), shape(RANK, 2 * FF), shape(RANK, FF), shape(RANK, width)),
        in_specs=[vmem] * 9,
        out_specs=(vmem,) * 4,
        scratch_shapes=[
            pltpu.VMEM((devices, count, width), jnp.bfloat16),
            pltpu.VMEM((devices, count, width), jnp.bfloat16),
            pltpu.SemaphoreType.DMA((2, devices)),
            pltpu.SemaphoreType.DMA((2, devices)),
        ],
        compiler_params=pltpu.CompilerParams(
            collective_id=0, has_side_effects=True, vmem_limit_bytes=56 * 1024 * 1024
        ),
        name="train",
    )(tokens, cotangent, weight, joined_weight, down_weight, a_in, b_in, a_out, b_out)
    return jnp.concatenate(
        [g_a_in.T.reshape(-1), g_b_in.reshape(-1), g_a_out.T.reshape(-1), g_b_out.reshape(-1)]
    )


def expert_decode(rows, joined_weight, down_weight, flat_bf):
    a_in, b_in, a_out, b_out = unpack(flat_bf)
    mid_in = product(rows, a_in).astype(jnp.bfloat16)
    joined = product(rows, joined_weight) + adapter_scale_factor * product(mid_in, b_in)
    gate = joined[:, :FF]
    hidden = (jax.nn.silu(gate) * joined[:, FF:]).astype(jnp.bfloat16)
    mid_out = product(hidden, a_out).astype(jnp.bfloat16)
    return (
        product(hidden, down_weight) + adapter_scale_factor * product(mid_out, b_out)
    ).astype(jnp.bfloat16)


def adamw(master, moment, second, grads):
    moment_new = beta_one * moment + (1.0 - beta_one) * grads
    second_new = beta_two * second + (1.0 - beta_two) * grads * grads
    step_size = moment_new / bias_one / (jnp.sqrt(second_new / bias_two) + epsilon)
    return master - learn_rate * (step_size + decay_rate * master)


def expert_weights(ids, weights, held_by):
    hit = ids[:, :, None] == held_by[None, None, :]
    return jnp.sum(jnp.where(hit, weights[:, :, None], 0.0), axis=1)


def exchange(array):
    return lax.all_to_all(array, "ep", split_axis=0, concat_axis=0, tiled=True)


def on_device(
    tokens,
    cotangent,
    route_ids,
    route_weights,
    owner,
    base_joined,
    base_down,
    master,
    moment,
    second,
    step_rows,
    step_ids,
    step_weights,
):
    experts = owner.shape[0]
    width = tokens.shape[1]
    me = lax.axis_index("ep")
    joined_weight = base_joined[0]
    down_weight = base_down[0]
    labels = jnp.arange(experts, dtype=jnp.int32)
    held_by = jnp.sum(jnp.where(owner[None, :] == labels[:, None], labels[None, :], 0), axis=1)
    steps, dec_rows = step_rows.shape[:2]

    def gather(array):
        return lax.all_gather(array, "ep", axis=0, tiled=True)

    my_weights = jnp.concatenate(
        [
            expert_weights(route_ids, route_weights, held_by),
            expert_weights(
                step_ids.reshape(steps * dec_rows, -1),
                step_weights.reshape(steps * dec_rows, -1),
                held_by,
            ),
        ]
    )
    all_weights = exchange(my_weights.T[:, None, :])[:, 0, :]
    tok_rows = tokens.shape[0]
    chunks = max(1, experts // 16)
    part = tok_rows // chunks
    flat_bf = exchange(jnp.take(master.astype(jnp.bfloat16), held_by, axis=0)).reshape(-1)
    all_steps = gather(step_rows.reshape(steps * dec_rows, width))
    if experts == 16:
        grads = train(
            tokens,
            cotangent,
            all_weights[:, :tok_rows, None],
            joined_weight,
            down_weight,
            flat_bf,
        )
    else:
        grads = 0.0
        for chunk in range(chunks):
            cut = slice(chunk * part, (chunk + 1) * part)
            all_tokens = gather(tokens[cut])
            all_cot = gather(cotangent[cut]).astype(jnp.float32)
            scaled = (all_weights[:, cut].reshape(-1, 1) * all_cot).astype(jnp.bfloat16)
            grads += expert_grads(all_tokens, scaled, joined_weight, down_weight, flat_bf)
    returned = exchange(grads.astype(jnp.bfloat16).reshape(experts, -1))
    my_grads = jnp.take(returned, owner, axis=0).astype(jnp.float32)
    updated = adamw(master, moment, second, my_grads)
    serving = exchange(jnp.take(updated.astype(jnp.bfloat16), held_by, axis=0)).reshape(-1)
    result = expert_decode(all_steps, joined_weight, down_weight, serving)
    back = exchange(result.reshape(experts, steps * dec_rows, width))
    mixed = jnp.sum(
        my_weights[tok_rows:].T[:, :, None] * back.astype(jnp.float32), axis=0
    )
    return (updated, mixed.astype(jnp.bfloat16).reshape(steps, dec_rows, width))


def solution(mesh):
    in_specs = (
        P(("grp", "ep"), None),
        P(("grp", "ep"), None),
        P(("grp", "ep"), None),
        P(("grp", "ep"), None),
        P("grp"),
        P("ep", None, None),
        P("ep", None, None),
        P("grp", "ep"),
        P("grp", "ep"),
        P("grp", "ep"),
        P(None, ("grp", "ep"), None),
        P(None, ("grp", "ep"), None),
        P(None, ("grp", "ep"), None),
    )
    out_specs = (P("grp", "ep"), P(None, ("grp", "ep"), None))
    return jax.shard_map(
        on_device, mesh=mesh, in_specs=in_specs, out_specs=out_specs, check_vma=False
    )
```

profile of v0, /device:TPU:0, one launch (start us, length us, event | category | flops | bytes accessed | tf_op | source)
XLA Modules:
  0.0 274.9 jit_solution(9232728197955712796)
XLA Ops:
  7.2 0.8 select_reduce_fusion.2
  7.9 0.8 copy.37
  8.7 0.8 copy.38
  9.6 0.8 select_reduce_fusion.1
  10.4 0.6 copy.39
  11.0 7.4 %all-to-all-start = ((f32[16,1,160]{2,1,0:T(1,128)}), f32[16,1,160]{2,1,0:T(1,128)S(1)}, u32[]{:S(2)}, u32[]{:S(2)}) async-start(f32[16,1,160]{2,1,0:T(1,128)} %copy.39), calls=%async_computation | async-start | bytes 32768 | tf_op jit(solution)/shard_map/all_to_all | solution.py:285
  18.5 1.1 convert_element_type.44
  19.6 0.8 gather_fusion
  20.4 0.1 select_bitcast_fusion.1
  20.5 0.5 broadcast.75
  21.0 0.8 reduce.6
  21.8 0.8 reshape.141
  22.6 2.3 all-to-all-done
  24.9 3.7 %all-to-all-start.1 = ((bf16[16,2,5248]{2,1,0:T(2,128)(2,1)}), bf16[16,2,5248]{2,1,0:T(2,128)(2,1)S(1)}, u32[]{:S(2)}, u32[]{:S(2)}) async-start(bf16[16,2,5248]{2,1,0:T(2,128)(2,1)} %reshape.141), calls=%async_computation.1 | async-start | bytes 671744 | tf_op jit(solution)/shard_map/all_to_all | solution.py:285
  28.7 1.4 copy.41.weight
  30.0 9.8 %all-to-all-done.1 = bf16[16,2,5248]{2,1,0:T(2,128)(2,1)S(1)} async-done(((bf16[16,2,5248]{2,1,0:T(2,128)(2,1)}), bf16[16,2,5248]{2,1,0:T(2,128)(2,1)S(1)}, u32[]{:S(2)}, u32[]{:S(2)}) %all-to-all-start.1) | async-done | bytes 335904 | tf_op jit(solution)/shard_map/all_to_all | solution.py:285
  39.9 0.3 reshape.142
  40.2 2.1 reduce
  42.3 0.5 reshape.92
  42.8 0.4 slice.52
  43.2 0.9 slice.48
  44.2 0.6 slice.71.a_out
  44.8 0.8 slice.69.a_in
  45.6 0.7 reshape.93.b_in
  46.3 0.7 slice.72.b_out
  47.0 93.8 %train.1 = (f32[32,2048]{1,0:T(8,128)}, f32[32,768]{1,0:T(8,128)}, f32[32,384]{1,0:T(8,128)}, f32[32,2048]{1,0:T(8,128)}) custom-call(bf16[128,2048]{1,0:T(8,128)(2,1)} %tok.1, bf16[128,2048]{1,0:T(8,128)(2,1)} %cot.1, f32[16,128,1]{2,1,0:T(8,128)} %copy.41.weight, bf16[2048,768]{1,0:T(8,128)(2,1)} %bitcast.45, bf16[384,2048]{1,0:T(8,128)(2,1)} %bitcast.44, ...), custom_call_target="tpu_custom_call" | custom-call | tf_op jit(solution)/shard_map/train/pallas_call | solution.py:239
  140.8 1.0 convert_bitcast_fusion.2
  141.8 0.8 convert_bitcast_fusion.3
  142.6 0.9 convert.19
  143.5 0.1 copy.43
  143.7 0.1 reshape.96
  143.8 1.0 convert_bitcast_fusion.1
  144.8 0.3 copy.42
  145.1 0.3 reshape.94
  145.4 0.2 convert_element_type.55
  145.6 2.6 reduce.7
  148.2 0.8 reshape.143
  149.0 3.8 %all-to-all-start.2 = ((bf16[16,2,5248]{2,1,0:T(2,128)(2,1)}), bf16[16,2,5248]{2,1,0:T(2,128)(2,1)S(1)}, u32[]{:S(2)}, u32[]{:S(2)}) async-start(bf16[16,2,5248]{2,1,0:T(2,128)(2,1)} %reshape.143), calls=%async_computation.2 | async-start | bytes 671744 | tf_op jit(solution)/shard_map/all_to_all | solution.py:285
  152.8 0.2 all-gather.2.cloned.1.call-start
  153.0 0.5 all-gather.2.cloned.1.call-update
  153.6 10.4 %all-to-all-done.2 = bf16[16,2,5248]{2,1,0:T(2,128)(2,1)S(1)} async-done(((bf16[16,2,5248]{2,1,0:T(2,128)(2,1)}), bf16[16,2,5248]{2,1,0:T(2,128)(2,1)S(1)}, u32[]{:S(2)}, u32[]{:S(2)}) %all-to-all-start.2) | async-done | bytes 335904 | tf_op jit(solution)/shard_map/all_to_all | solution.py:285
  164.0 0.3 reshape.144
  164.4 0.8 gather_fusion.1
  165.1 0.3 copy-done.2
  165.4 0.2 copy-done.3
  165.6 0.2 copy-done.4
  165.8 1.5 fusion.20
  167.3 0.8 gather_fusion.2
  168.2 0.8 reduce.8
  169.1 14.9 %all_to_all.37 = bf16[16,2,5248]{2,1,0:T(2,128)(2,1)S(1)} all-to-all(bf16[16,2,5248]{2,1,0:T(2,128)(2,1)S(1)} %reshape.145), channel_id=1, replica_groups=mesh['grp'=2,'ep'=16] {'ep'}, dimensions={0} | all-to-all | bytes 671744 | tf_op jit(solution)/shard_map/all_to_all | solution.py:285
  184.0 1.0 reshape.146
  185.0 3.1 %reduce.3 = bf16[16,10496]{1,0:T(8,128)(2,1)S(1)} reduce(bf16[16,1,10496]{2,1,0:T(2,128)(2,1)} %reshape.146, bf16[]{:T(256)} %constant.43), dimensions={1}, to_apply=%all_to_all.30.reduce_sub_computation | reduce | bytes 671746 | tf_op jit(solution)/shard_map/all_to_all | solution.py:285
  188.1 1.3 reshape.99
  189.4 1.2 slice.60
  190.6 2.0 slice.54
  192.6 7.8 %all-gather.2.cloned.1.call-done = bf16[512,2048]{1,0:T(8,128)(2,1)} async-done(((bf16[32,2048]{1,0:T(8,128)(2,1)}), bf16[512,2048]{1,0:T(8,128)(2,1)}) %all-gather.2.cloned.1.call-update) | async-done | bytes 2097168 | tf_op jit(solution)/shard_map/all_gather | solution.py:313
  200.5 4.5 %fusion.18 = f32[512,768]{1,0:T(8,128)} fusion(bf16[512,2048]{1,0:T(8,128)(2,1)} %all-gather.2.cloned.1.call-done, bf16[1,2048,768]{2,1,0:T(8,128)(2,1)S(1)} %copy-done.1), kind=kOutput, calls=%fused_computation.48 | convolution fusion | flops 1610612736 | bytes 6815744 | tf_op jit(solution)/shard_map/dot_general | solution.py:24
  205.0 3.4 %multiply_add_fusion = f32[512,768]{1,0:T(8,128)S(1)} fusion(f32[512,768]{1,0:T(8,128)} %fusion.18, bf16[32,768]{1,0:T(8,128)(2,1)S(1)} %reshape.100, bf16[512,2048]{1,0:T(8,128)(2,1)} %all-gather.2.cloned.1.call-done, bf16[5248,32]{1,0:T(8,128)(2,1)} %slice.54), kind=kOutput, calls=%fused_computation.5 | convolution fusion | flops 93077504 | bytes 5816320 | tf_op jit(solution)/shard_map/dot_general | solution.py:24
  208.4 0.2 fusion
  208.6 1.2 copy-done
  209.8 3.2 %fusion.16 = f32[512,2048]{1,0:T(8,128)} fusion(bf16[512,384]{1,0:T(8,128)(2,1)S(1)} %fusion, bf16[1,384,2048]{2,1,0:T(8,128)(2,1)S(1)} %copy-done), kind=kOutput, calls=%fused_computation.46 | convolution fusion | flops 805306368 | bytes 6160384 | tf_op jit(solution)/shard_map/dot_general | solution.py:24
  213.0 3.3 %add_convert_fusion = bf16[512,2048]{1,0:T(8,128)(2,1)S(1)} fusion(f32[512,2048]{1,0:T(8,128)} %fusion.16, bf16[512,384]{1,0:T(8,128)(2,1)S(1)} %fusion, bf16[82,2048]{1,0:T(8,128)(2,1)} %slice.60, bf16[5248,32]{1,0:T(8,128)(2,1)} %slice.54), kind=kOutput, calls=%fused_computation.4 | convolution fusion | flops 82853888 | bytes 6914048 | tf_op jit(solution)/shard_map/dot_general | solution.py:24
  216.3 50.6 %all_to_all.38 = bf16[16,32,2048]{2,1,0:T(8,128)(2,1)S(1)} all-to-all(bf16[16,32,2048]{2,1,0:T(8,128)(2,1)S(1)} %bitcast.43), channel_id=1, replica_groups=mesh['grp'=2,'ep'=16] {'ep'}, dimensions={0} | all-to-all | bytes 4194304 | tf_op jit(solution)/shard_map/all_to_all | solution.py:285
  266.9 1.2 multiply_reduce_fusion
  (28 shorter events, 0.6 us)
Async XLA Ops:
  11.0 13.9 %all-to-all-start = ((f32[16,1,160]{2,1,0:T(1,128)}), f32[16,1,160]{2,1,0:T(1,128)S(1)}, u32[]{:S(2)}, u32[]{:S(2)}) async-start(f32[16,1,160]{2,1,0:T(1,128)} %copy.39), calls=%async_computation | async-start | bytes 32768 | tf_op jit(solution)/shard_map/all_to_all | solution.py:285
  24.9 15.0 %all-to-all-start.1 = ((bf16[16,2,5248]{2,1,0:T(2,128)(2,1)}), bf16[16,2,5248]{2,1,0:T(2,128)(2,1)S(1)}, u32[]{:S(2)}, u32[]{:S(2)}) async-start(bf16[16,2,5248]{2,1,0:T(2,128)(2,1)} %reshape.141), calls=%async_computation.1 | async-start | bytes 671744 | tf_op jit(solution)/shard_map/all_to_all | solution.py:285
  145.3 8.2 %copy-start.5 = (s32[16]{0:T(128)S(1)}, s32[16]{0:T(128)}, u32[]{:S(2)}) copy-start(s32[16]{0:T(128)} %param.19) | copy-start | bytes 196
  149.0 15.0 %all-to-all-start.2 = ((bf16[16,2,5248]{2,1,0:T(2,128)(2,1)}), bf16[16,2,5248]{2,1,0:T(2,128)(2,1)S(1)}, u32[]{:S(2)}, u32[]{:S(2)}) async-start(bf16[16,2,5248]{2,1,0:T(2,128)(2,1)} %reshape.143), calls=%async_computation.2 | async-start | bytes 671744 | tf_op jit(solution)/shard_map/all_to_all | solution.py:285
  152.8 47.7 %all-gather.2.cloned.1.call-start = ((), (), s32[]{:S(2)}) async-start(), calls=%async_computation.5 | async-start | bytes 2228224 | tf_op jit(solution)/shard_map/all_gather | solution.py:313
  164.3 1.1 copy-start.2
  164.3 1.3 copy-start.3
  164.3 1.5 copy-start.4
  185.0 15.5 %copy-start.1 = (bf16[1,2048,768]{2,1,0:T(8,128)(2,1)S(1)}, bf16[1,2048,768]{2,1,0:T(8,128)(2,1)}, u32[]{:S(2)}) copy-start(bf16[1,2048,768]{2,1,0:T(8,128)(2,1)} %param.20) | copy-start | bytes 9437188
  189.4 3.2 %slice-start = ((bf16[167936]{0:T(1024)(128)(2,1)}), bf16[24576]{0:T(1024)(128)(2,1)S(1)}, s32[]{:S(2)}) async-start(bf16[167936]{0:T(1024)(128)(2,1)} %reshape.99), calls=%async_computation.6 | async-start | bytes 98304 | tf_op jit(solution)/shard_map/slice | solution.py:32
  208.4 1.4 copy-start
Sparse Core Ops, SparseCore 0:
  155.8 44.6 all-gather.1
where the time goes:
time: 276 us; the launch traced here: 275 us
  Pallas kernels  93.8 us (34%)
  blocking collectives  65.5 us (24%)
  waiting for transfers between devices  30.9 us (11%)
  local copies, waits for them, and re-layouts  21.9 us (8%)
  other arithmetic  19 us (7%)
  starting transfers between devices  15.1 us (5%)
  matrix products  14.4 us (5%)
  between operations  14.4 us (5%)
    pallas_call x1, Pallas kernels, train(): pl.pallas_call(train_kernel, out_shape=(shape(RANK, width), shape(RANK, 2...  93.8 us
    all_to_all x2, blocking collectives, exchange(): return lax.all_to_all(array, 'ep', split_axis=0, concat_axis=0, tiled=True)  65.5 us
    all_to_all x3, waiting for transfers between devices, exchange(): return lax.all_to_all(array, 'ep', split_axis=0, concat_axis=0, tiled=True)  22.6 us
    all_to_all x3, starting transfers between devices, exchange(): return lax.all_to_all(array, 'ep', split_axis=0, concat_axis=0, tiled=True)  14.9 us
    dot_general x4, matrix products, product(): return jnp.dot(left, right, preferred_element_type=jnp.float32)  14.4 us
    all_gather x1, waiting for transfers between devices, gather(): return lax.all_gather(array, 'ep', axis=0, tiled=True)  7.83 us
    all_to_all x6, other arithmetic, exchange(): return lax.all_to_all(array, 'ep', split_axis=0, concat_axis=0, tiled=True)  7.06 us
  transfers between devices with their start and end apart: 4, of which 4 were waited for; matrix products, arithmetic and copies ran while one was open for 7% of the time, Pallas kernels for 0%

commit v1 on v0

--- a/solution.py
+++ b/solution.py
@@ -257,6 +257,401 @@
     )
 
 
+def snake(devices):
+    chips = devices // 2
+    half = chips // 2
+    me = lax.axis_index("ep")
+    core = lax.rem(me, 2)
+    chip = me // 2
+    place = jnp.where(lax.rem(chip, 2) == 0, chip // 2, chips - 1 - chip // 2)
+
+    def chip_at(position):
+        position = lax.rem(position + 2 * chips, chips)
+        return jnp.where(position < half, 2 * position, 2 * (chips - 1 - position) + 1)
+
+    return me, core, chip, place, chip_at
+
+
+def spread(block):
+    pieces = []
+    for start in range(0, block.shape[0], 128):
+        cut = block[start : start + 128]
+        count = cut.shape[0]
+        shape = (4 * count, count)
+        rows = lax.broadcasted_iota(jnp.int32, shape, 0)
+        repeat = (rows // 4 == lax.broadcasted_iota(jnp.int32, shape, 1)).astype(jnp.bfloat16)
+        wide = product(repeat, cut)
+        shape = (4 * count, 128)
+        rows = lax.broadcasted_iota(jnp.int32, shape, 0)
+        lanes = lax.broadcasted_iota(jnp.int32, shape, 1)
+        wide = jnp.where(lanes // RANK == lax.rem(rows, 4), wide, 0.0).astype(jnp.bfloat16)
+        shape = (128, RANK)
+        lanes = lax.broadcasted_iota(jnp.int32, shape, 0)
+        fold = (lax.rem(lanes, RANK) == lax.broadcasted_iota(jnp.int32, shape, 1)).astype(
+            jnp.bfloat16
+        )
+        pieces.append(product(wide, fold).astype(jnp.bfloat16))
+    return jnp.concatenate(pieces, axis=0)
+
+
+def weave(block):
+    count = block.shape[0]
+    times = count // RANK
+    shape = (count, count)
+    rows = lax.broadcasted_iota(jnp.int32, shape, 0)
+    source = lax.rem(rows, RANK) * times + rows // RANK
+    pick = (source == lax.broadcasted_iota(jnp.int32, shape, 1)).astype(jnp.bfloat16)
+    sorted_rows = product(pick, block).astype(jnp.bfloat16)
+    return jnp.concatenate(
+        [sorted_rows[RANK * j : RANK * (j + 1)] for j in range(times)], axis=1
+    )
+
+
+def restore(pieces, flat, factors):
+    count = pieces.shape[1]
+    for j in range(pieces.shape[0]):
+        flat[count * j : count * (j + 1), :] = pieces[j].astype(jnp.float32)
+    cuts = [0]
+    for size in (D * RANK, RANK * 2 * FF, FF * RANK, RANK * D):
+        cuts.append(cuts[-1] + size // 128)
+    for k, undo in enumerate((spread, weave, spread, weave)):
+        factors[k][...] = undo(flat[cuts[k] : cuts[k + 1], :].astype(jnp.bfloat16))
+
+
+def serve_kernel(
+    owner,
+    held_by,
+    grads,
+    master,
+    moment,
+    second,
+    rows_in,
+    weight,
+    wf,
+    wd,
+    updated,
+    decoded,
+    got_grads,
+    fresh,
+    serving,
+    pieces,
+    flat,
+    a_in,
+    b_in,
+    a_out,
+    b_out,
+    held,
+    base,
+    keep,
+    give,
+    got,
+    out_buf,
+    in_buf,
+    piece_send,
+    piece_recv,
+    row_send,
+    row_recv,
+    give_send,
+    give_recv,
+    sum_send,
+    sum_recv,
+):
+    devices = lax.axis_size("ep")
+    half = devices // 4
+    me, core, chip, place, chip_at = snake(devices)
+    right = 2 * chip_at(place + 1) + core
+    left = 2 * chip_at(place - 1) + core
+    sibling = 2 * chip + 1 - core
+    count = rows_in.shape[0]
+    part = count // 2
+
+    barrier = pltpu.get_barrier_semaphore()
+
+    def greet(k, carry):
+        pl.semaphore_signal(
+            barrier,
+            inc=1,
+            device_id={"ep": lax.rem(me + k, devices)},
+            device_id_type=pl.DeviceIdType.MESH,
+        )
+        return carry
+
+    lax.fori_loop(1, devices, greet, 0)
+    pl.semaphore_wait(barrier, devices - 1)
+
+    def remote(source, target, send, recv, other):
+        return pltpu.make_async_remote_copy(
+            src_ref=source,
+            dst_ref=target,
+            send_sem=send,
+            recv_sem=recv,
+            device_id={"ep": other},
+            device_id_type=pl.DeviceIdType.MESH,
+        )
+
+    def piece_to(kind, source, target, other):
+        return remote(
+            source.at[other],
+            target.at[me],
+            piece_send.at[kind, other],
+            piece_recv.at[kind, me],
+            other,
+        )
+
+    def piece_from(kind, source, target, other):
+        return remote(
+            source.at[other],
+            target.at[other],
+            piece_send.at[kind, other],
+            piece_recv.at[kind, other],
+            other,
+        )
+
+    def each_other(act):
+        def body(k, carry):
+            act(lax.rem(me + k, devices))
+            return carry
+
+        lax.fori_loop(1, devices, body, 0)
+
+    each_other(lambda other: piece_to(0, grads, got_grads, other).start())
+
+    def cut(slot, kind):
+        return held.at[slot, pl.ds(part * kind, part)]
+
+    def row_move(source, slot, kind, other):
+        return remote(
+            source, cut(slot, kind), row_send.at[kind, slot], row_recv.at[kind, slot], other
+        )
+
+    def row_arrived(slot, kind):
+        row_move(cut(slot, kind), slot, kind, sibling).wait_recv()
+
+    for kind in (0, 1):
+        own = rows_in.at[pl.ds(part * kind, part)]
+        row_move(own, 4, kind, right).start()
+        row_move(own, 5, kind, left).start()
+        row_move(own, 2, kind, sibling).start()
+    held[0] = rows_in[...]
+    got_grads[me] = grads[me]
+    each_other(lambda other: piece_from(0, grads, got_grads, other).wait_recv())
+
+    def renew(k, carry):
+        other = lax.rem(me + k, devices)
+        expert = held_by[other]
+        fresh[other] = adamw(
+            master[expert], moment[expert], second[expert], got_grads[other].astype(jnp.float32)
+        )
+        serving[other] = fresh[other].astype(jnp.bfloat16)
+
+        @pl.when(k < devices)
+        def _():
+            piece_to(1, serving, pieces, other).start()
+
+        return carry
+
+    lax.fori_loop(1, devices + 1, renew, 0)
+    pieces[me] = serving[me]
+
+    def row_step(s, carry):
+        for kind in (0, 1):
+            for way, onward in ((0, right), (1, left)):
+                slot = 4 * s + way
+                row_arrived(slot, kind)
+
+                @pl.when(s < half - 1)
+                def _():
+                    row_move(cut(slot, kind), slot + 4, kind, onward).start()
+
+                if way == kind:
+
+                    @pl.when(s == half - 1)
+                    def _():
+                        row_move(cut(slot, kind), 1, kind, onward).start()
+
+                row_move(cut(slot, kind), slot + 2, kind, sibling).start()
+        return carry
+
+    lax.fori_loop(1, half, row_step, 0)
+
+    def write_back(expert, carry):
+        updated[expert] = fresh[owner[expert]]
+        return carry
+
+    lax.fori_loop(0, devices, write_back, 0)
+    for kind in (0, 1):
+        row_arrived(1, kind)
+        row_move(cut(1, kind), 3, kind, sibling).start()
+
+    def rest(slot, carry):
+        for kind in (0, 1):
+            row_arrived(slot, kind)
+        return carry
+
+    lax.fori_loop(2, 4, rest, 0)
+    for s in range(1, half):
+        lax.fori_loop(4 * s + 2, 4 * s + 4, rest, 0)
+
+    def base_of(tile, carry):
+        rows = held[pl.ds(8 * tile, 8)].reshape(8 * count, rows_in.shape[1])
+        base[tile] = product(rows, wf[...])
+        return carry
+
+    lax.fori_loop(0, devices // 8, base_of, 0)
+    each_other(lambda other: piece_from(1, serving, pieces, other).wait_recv())
+    restore(pieces, flat, (a_in, b_in, a_out, b_out))
+
+    def answer(k, carry):
+        s = jnp.where(k == 0, 0, half - k)
+        rows = held[pl.ds(4 * s, 4)].reshape(4 * count, rows_in.shape[1])
+        mid_in = product(rows, a_in[...]).astype(jnp.bfloat16)
+        from_base = base[s // 2, pl.ds(lax.rem(s, 2) * 4 * count, 4 * count), :]
+        joined = from_base + adapter_scale_factor * product(mid_in, b_in[...])
+        gate = joined[:, :FF]
+        hidden = (gate * jax.nn.sigmoid(gate) * joined[:, FF:]).astype(jnp.bfloat16)
+        mid_out = product(hidden, a_out[...]).astype(jnp.bfloat16)
+        result = product(hidden, wd[...]) + adapter_scale_factor * product(mid_out, b_out[...])
+        result = result.astype(jnp.bfloat16).astype(jnp.float32)
+        first = 2 * chip_at(place - s)
+        second_chip = 2 * chip_at(place + jnp.where(s == 0, half, s))
+        gains = jnp.concatenate(
+            [
+                weight[first + core],
+                weight[second_chip + core],
+                weight[first + 1 - core],
+                weight[second_chip + 1 - core],
+            ],
+            axis=0,
+        )
+        result = (gains * result).reshape(4, count, rows_in.shape[1])
+        keep[s] = result[:2]
+        give[s] = result[2:].astype(jnp.bfloat16)
+        remote(give.at[s], got.at[s], give_send.at[s], give_recv.at[s], sibling).start()
+        return carry
+
+    lax.fori_loop(0, half, answer, 0)
+
+    def sum_move(way, t, piece, other):
+        spot = pl.ds(part * piece, part)
+        return remote(
+            out_buf.at[way, t, spot],
+            in_buf.at[way, t, spot],
+            sum_send.at[way, t, piece],
+            sum_recv.at[way, t, piece],
+            other,
+        )
+
+    def got_wait(s):
+        remote(give.at[s], got.at[s], give_send.at[s], give_recv.at[s], sibling).wait_recv()
+
+    def of_chip(s, way):
+        return keep[s, way] + got[s, way].astype(jnp.float32)
+
+    got_wait(0)
+    opposite = of_chip(0, 1).astype(jnp.bfloat16)
+    for way, onward in ((0, right), (1, left)):
+        out_buf[way, 0, part * way : part * (way + 1), :] = opposite[part * way : part * (way + 1)]
+        sum_move(way, 0, way, onward).start()
+    for t in range(1, half):
+        s = half - t
+        got_wait(s)
+        for way, onward in ((0, right), (1, left)):
+            total = of_chip(s, 1 - way)
+            for piece in (0, 1):
+                low, high = part * piece, part * (piece + 1)
+                term = total[low:high]
+                if t > 1 or piece == way:
+                    sum_move(way, t - 1, piece, onward).wait_recv()
+                    term = term + in_buf[way, t - 1, low:high, :].astype(jnp.float32)
+                out_buf[way, t, low:high, :] = term.astype(jnp.bfloat16)
+                sum_move(way, t, piece, onward).start()
+    total = of_chip(0, 0)
+    for way in (0, 1):
+        for piece in (0, 1):
+            sum_move(way, half - 1, piece, left).wait_recv()
+        total = total + in_buf[way, half - 1].astype(jnp.float32)
+    decoded[...] = total.astype(jnp.bfloat16)
+
+    def piece_sent(other):
+        piece_to(0, grads, got_grads, other).wait_send()
+        piece_to(1, serving, pieces, other).wait_send()
+
+    each_other(piece_sent)
+
+    def rows_sent(slot, carry):
+        for kind in (0, 1):
+            row_move(cut(slot, kind), slot, kind, sibling).wait_send()
+        return carry
+
+    lax.fori_loop(1, devices, rows_sent, 0)
+    for s in range(half):
+        remote(give.at[s], got.at[s], give_send.at[s], give_recv.at[s], sibling).wait_send()
+    for way in (0, 1):
+        for t in range(half):
+            for piece in (0, 1):
+                if t > 0 or piece == way:
+                    sum_move(way, t, piece, left).wait_send()
+
+
+def serve(owner, held_by, grads, master, moment, second, rows, weight, joined_weight, down_weight):
+    devices = lax.axis_size("ep")
+    half = devices // 4
+    count, width = rows.shape
+    lane_rows = master.shape[1] // 128
+    cube = (devices, lane_rows, 128)
+    vmem = pl.BlockSpec(memory_space=pltpu.VMEM)
+    smem = pl.BlockSpec(memory_space=pltpu.SMEM)
+    bf, f32 = jnp.bfloat16, jnp.float32
+    updated, decoded = pl.pallas_call(
+        serve_kernel,
+        out_shape=(jax.ShapeDtypeStruct(cube, f32), jax.ShapeDtypeStruct((count, width), bf)),
+        in_specs=[smem] * 2 + [vmem] * 8,
+        out_specs=(vmem,) * 2,
+        scratch_shapes=[
+            pltpu.VMEM(cube, bf),
+            pltpu.VMEM(cube, f32),
+            pltpu.VMEM(cube, bf),
+            pltpu.VMEM(cube, bf),
+            pltpu.VMEM((devices * lane_rows, 128), f32),
+            pltpu.VMEM((width, RANK), bf),
+            pltpu.VMEM((RANK, 2 * FF), bf),
+            pltpu.VMEM((FF, RANK), bf),
+            pltpu.VMEM((RANK, width), bf),
+            pltpu.VMEM((devices, count, width), bf),
+            pltpu.VMEM((devices // 8, 8 * count, 2 * FF), f32),
+            pltpu.VMEM((half, 2, count, width), f32),
+            pltpu.VMEM((half, 2, count, width), bf),
+            pltpu.VMEM((half, 2, count, width), bf),
+            pltpu.VMEM((2, half, count, width), bf),
+            pltpu.VMEM((2, half, count, width), bf),
+            pltpu.SemaphoreType.DMA((2, devices)),
+            pltpu.SemaphoreType.DMA((2, devices)),
+            pltpu.SemaphoreType.DMA((2, devices)),
+            pltpu.SemaphoreType.DMA((2, devices)),
+            pltpu.SemaphoreType.DMA((half,)),
+            pltpu.SemaphoreType.DMA((half,)),
+            pltpu.SemaphoreType.DMA((2, half, 2)),
+            pltpu.SemaphoreType.DMA((2, half, 2)),
+        ],
+        compiler_params=pltpu.CompilerParams(
+            collective_id=1, has_side_effects=True, vmem_limit_bytes=56 * 1024 * 1024
+        ),
+        name="serve",
+    )(
+        owner,
+        held_by,
+        grads.astype(bf).reshape(cube),
+        master.reshape(cube),
+        moment.reshape(cube),
+        second.reshape(cube),
+        rows,
+        weight,
+        joined_weight,
+        down_weight,
+    )
+    return updated.reshape(master.shape), decoded
+
+
 def expert_decode(rows, joined_weight, down_weight, flat_bf):
     a_in, b_in, a_out, b_out = unpack(flat_bf)
     mid_in = product(rows, a_in).astype(jnp.bfloat16)
@@ -327,7 +722,6 @@
     chunks = max(1, experts // 16)
     part = tok_rows // chunks
     flat_bf = exchange(jnp.take(master.astype(jnp.bfloat16), held_by, axis=0)).reshape(-1)
-    all_steps = gather(step_rows.reshape(steps * dec_rows, width))
     if experts == 16:
         grads = train(
             tokens,
@@ -337,14 +731,27 @@
             down_weight,
             flat_bf,
         )
-    else:
-        grads = 0.0
-        for chunk in range(chunks):
-            cut = slice(chunk * part, (chunk + 1) * part)
-            all_tokens = gather(tokens[cut])
-            all_cot = gather(cotangent[cut]).astype(jnp.float32)
-            scaled = (all_weights[:, cut].reshape(-1, 1) * all_cot).astype(jnp.bfloat16)
-            grads += expert_grads(all_tokens, scaled, joined_weight, down_weight, flat_bf)
+        updated, decoded = serve(
+            owner,
+            held_by,
+            grads,
+            master,
+            moment,
+            second,
+            step_rows.reshape(steps * dec_rows, width),
+            all_weights[:, tok_rows:, None],
+            joined_weight,
+            down_weight,
+        )
+        return (updated, decoded.reshape(steps, dec_rows, width))
+    grads = 0.0
+    for chunk in range(chunks):
+        cut = slice(chunk * part, (chunk + 1) * part)
+        all_tokens = gather(tokens[cut])
+        all_cot = gather(cotangent[cut]).astype(jnp.float32)
+        scaled = (all_weights[:, cut].reshape(-1, 1) * all_cot).astype(jnp.bfloat16)
+        grads += expert_grads(all_tokens, scaled, joined_weight, down_weight, flat_bf)
+    all_steps = gather(step_rows.reshape(steps * dec_rows, width))
     returned = exchange(grads.astype(jnp.bfloat16).reshape(experts, -1))
     my_grads = jnp.take(returned, owner, axis=0).astype(jnp.float32)
     updated = adamw(master, moment, second, my_grads)

time: 276 us -> 205 us (0.74)
  blocking collectives: 65.5 us -> 0 us
  Pallas kernels: 93.8 us -> 157 us
  waiting for transfers between devices: 30.9 us -> 8.19 us
  matrix products: 14.4 us -> 0 us
  between operations: 14.4 us -> 0.9 us
  other arithmetic: 19 us -> 6.98 us
  starting transfers between devices: 15.1 us -> 11.4 us
    all_to_all x2 -> x0, blocking collectives: 65.5 us -> none  [exchange(): return lax.all_to_all(array, 'ep', split_axis=0, concat_axis=0, tiled=True)]
    pallas_call x0 -> x1, Pallas kernels: none -> 63 us  [serve(): pl.pallas_call(serve_kernel, out_shape=(jax.ShapeDtypeStruct(cube, f32),...]
    dot_general x4 -> x0, matrix products: 14.4 us -> none  [product(): return jnp.dot(left, right, preferred_element_type=jnp.float32)]
    all_to_all x3 -> x2, waiting for transfers between devices: 22.6 us -> 8.19 us  [exchange(): return lax.all_to_all(array, 'ep', split_axis=0, concat_axis=0, tiled=True)]
    all_gather x1 -> x0, waiting for transfers between devices: 7.83 us -> none  [gather(): return lax.all_gather(array, 'ep', axis=0, tiled=True)]
    all_to_all x6 -> x1, other arithmetic: 7.06 us -> 2.08 us  [exchange(): return lax.all_to_all(array, 'ep', split_axis=0, concat_axis=0, tiled=True)]
    convert_element_type x3 -> x0, other arithmetic: 4.3 us -> none  [the longest x1 2.59 us: on_device(): returned = exchange(grads.astype(jnp.bfloat16).reshape(experts, -1))]
    all_to_all x3 -> x2, starting transfers between devices: 14.9 us -> 11.4 us  [exchange(): return lax.all_to_all(array, 'ep', split_axis=0, concat_axis=0, tiled=True)]
  transfers between devices with their start and end apart: 4 -> 2, of which waited for: 4 -> 2; matrix products, arithmetic and copies ran while one was open for 7% -> 5% of each run, Pallas kernels for 0% -> 0%
where the time goes in v1:
time: 205 us; the launch traced here: 204 us
  Pallas kernels  157 us (77%)
  local copies, waits for them, and re-layouts  19.9 us (10%)
  starting transfers between devices  11.4 us (6%)
  waiting for transfers between devices  8.19 us (4%)
  other arithmetic  6.98 us (3%)
    pallas_call x1, Pallas kernels, train(): pl.pallas_call(train_kernel, out_shape=(shape(RANK, width), shape(RANK, 2...  93.9 us
    pallas_call x1, Pallas kernels, serve(): pl.pallas_call(serve_kernel, out_shape=(jax.ShapeDtypeStruct(cube, f32),...  63 us
    all_to_all x2, starting transfers between devices, exchange(): return lax.all_to_all(array, 'ep', split_axis=0, concat_axis=0, tiled=True)  11.4 us
    all_to_all x2, waiting for transfers between devices, exchange(): return lax.all_to_all(array, 'ep', split_axis=0, concat_axis=0, tiled=True)  8.19 us
    unnamed x20, local copies, waits for them, and re-layouts  4.79 us
  transfers between devices with their start and end apart: 2, of which 2 were waited for; matrix products, arithmetic and copies ran while one was open for 5% of the time, Pallas kernels for 0%

profile of v1, /device:TPU:0, one launch (start us, length us, event | category | flops | bytes accessed | tf_op | source)
XLA Modules:
  0.0 204.2 jit_solution(12314438787459891532)
XLA Ops:
  0.6 0.8 select_reduce_fusion.2.held_by
  1.4 0.0 copy-start.6
  1.4 0.8 copy.43
  2.2 0.8 copy.44
  3.0 0.1 select_reduce_fusion
  3.1 0.8 select_reduce_fusion.1
  3.9 0.6 copy.45
  4.5 7.4 %all-to-all-start = ((f32[16,1,160]{2,1,0:T(1,128)}), f32[16,1,160]{2,1,0:T(1,128)S(1)}, u32[]{:S(2)}, u32[]{:S(2)}) async-start(f32[16,1,160]{2,1,0:T(1,128)} %copy.45), calls=%async_computation | async-start | bytes 32768 | tf_op jit(solution)/shard_map/all_to_all | solution.py:680
  11.9 1.1 convert_element_type.8
  13.1 0.8 gather_fusion
  13.8 0.0 copy-done.6
  13.8 0.0 copy-start
  13.8 0.1 bitcast_select_fusion
  14.0 0.5 broadcast.65
  14.5 0.0 copy-start.1
  14.5 0.9 reduce.3
  15.4 0.8 reshape.129
  16.2 0.0 copy-start.2
  16.2 2.2 %all-to-all-done = f32[16,1,160]{2,1,0:T(1,128)S(1)} async-done(((f32[16,1,160]{2,1,0:T(1,128)}), f32[16,1,160]{2,1,0:T(1,128)S(1)}, u32[]{:S(2)}, u32[]{:S(2)}) %all-to-all-start) | async-done | bytes 10272 | tf_op jit(solution)/shard_map/all_to_all | solution.py:680
  18.4 4.0 %all-to-all-start.1 = ((bf16[16,2,5248]{2,1,0:T(2,128)(2,1)}), bf16[16,2,5248]{2,1,0:T(2,128)(2,1)S(1)}, u32[]{:S(2)}, u32[]{:S(2)}) async-start(bf16[16,2,5248]{2,1,0:T(2,128)(2,1)} %reshape.129), calls=%async_computation.1 | async-start | bytes 671744 | tf_op jit(solution)/shard_map/all_to_all | solution.py:680
  22.4 0.0 copy-done
  22.4 1.0 reshape.112.master
  23.4 0.0 copy-done.1
  23.4 1.0 reshape.113.moment
  24.3 0.0 copy-done.2
  24.4 1.0 reshape.114.second
  25.3 1.4 copy.47.weight
  26.7 0.9 copy.50.weight
  27.6 6.0 %all-to-all-done.1 = bf16[16,2,5248]{2,1,0:T(2,128)(2,1)S(1)} async-done(((bf16[16,2,5248]{2,1,0:T(2,128)(2,1)}), bf16[16,2,5248]{2,1,0:T(2,128)(2,1)S(1)}, u32[]{:S(2)}, u32[]{:S(2)}) %all-to-all-start.1) | async-done | bytes 335904 | tf_op jit(solution)/shard_map/all_to_all | solution.py:680
  33.6 0.3 reshape.130
  33.9 2.1 %reduce = bf16[16,10496]{1,0:T(8,128)(2,1)S(1)} reduce(bf16[16,1,10496]{2,1,0:T(2,128)(2,1)S(1)} %reshape.130, bf16[]{:T(256)} %constant.24), dimensions={1}, to_apply=%all_to_all.8.reduce_sub_computation | reduce | bytes 671746 | tf_op jit(solution)/shard_map/all_to_all | solution.py:680
  36.0 0.9 slice.26
  36.9 0.8 slice.36.a_in
  37.7 0.6 slice.38.a_out
  38.4 0.4 slice.30
  38.8 0.5 reshape.106
  39.3 0.7 slice.39.b_out
  40.0 0.7 reshape.107.b_in
  40.7 93.9 %train.1 = (f32[32,2048]{1,0:T(8,128)}, f32[32,768]{1,0:T(8,128)}, f32[32,384]{1,0:T(8,128)}, f32[32,2048]{1,0:T(8,128)}) custom-call(bf16[128,2048]{1,0:T(8,128)(2,1)} %tok.1, bf16[128,2048]{1,0:T(8,128)(2,1)} %cot.1, f32[16,128,1]{2,1,0:T(8,128)} %copy.47.weight, bf16[2048,768]{1,0:T(8,128)(2,1)} %bitcast.34, bf16[384,2048]{1,0:T(8,128)(2,1)} %bitcast.36, ...), custom_call_target="tpu_custom_call" | custom-call | tf_op jit(solution)/shard_map/train/pallas_call | solution.py:239
  134.6 0.0 copy-start.3
  134.6 0.0 copy-start.5
  134.6 0.0 copy-start.4
  134.6 1.0 convert_bitcast_fusion.1
  135.7 0.3 copy.48
  135.9 0.3 reshape.108
  136.2 0.0 copy-done.3
  136.3 0.0 copy-done.5
  136.3 0.1 copy.49
  136.4 0.1 reshape.110
  136.6 0.0 copy-done.4
  136.6 0.1 reshape.109
  136.7 0.8 convert_element_type.9.grads
  137.5 63.0 %serve.1 = (f32[16,82,128]{2,1,0:T(8,128)}, bf16[32,2048]{1,0:T(8,128)(2,1)}) custom-call(s32[16]{0:T(128)} %owner.1, s32[16]{0:T(128)} %copy-done.6, bf16[16,82,128]{2,1,0:T(8,128)(2,1)} %convert_element_type.9.grads, f32[16,82,128]{2,1,0:T(8,128)} %reshape.112.master, f32[16,82,128]{2,1,0:T(8,128)} %reshape.113.moment, f32[16,82,128]{2,1,0:T(8,128)} %reshape.114.second, ...), custom_call_target="tpu_custom_call" | custom-call | tf_op jit(solution)/shard_map/serve/pallas_call | solution.py:605
  200.5 2.1 %copy.56 = f32[2,8,82,128]{3,1,2,0:T(8,128)} copy(f32[2,8,82,128]{3,2,1,0:T(8,128)} %bitcast.38) | data formatting | bytes 1343488
  202.6 1.6 copy.60
  (13 shorter events, 0.1 us)
Async XLA Ops:
  1.4 12.4 %copy-start.6 = (s32[16]{0:T(128)}, s32[16]{0:T(128)S(1)}, u32[]{:S(2)}) copy-start(s32[16]{0:T(128)S(1)} %select_reduce_fusion.2.held_by) | copy-start | bytes 196
  4.5 13.9 %all-to-all-start = ((f32[16,1,160]{2,1,0:T(1,128)}), f32[16,1,160]{2,1,0:T(1,128)S(1)}, u32[]{:S(2)}, u32[]{:S(2)}) async-start(f32[16,1,160]{2,1,0:T(1,128)} %copy.45), calls=%async_computation | async-start | bytes 32768 | tf_op jit(solution)/shard_map/all_to_all | solution.py:680
  13.8 8.5 %copy-start = (f32[16,10496]{1,0:T(8,128)S(1)}, f32[16,10496]{1,0:T(8,128)}, u32[]{:S(2)}) copy-start(f32[16,10496]{1,0:T(8,128)} %param.20) | copy-start | bytes 2015236
  14.5 8.9 %copy-start.1 = (f32[16,10496]{1,0:T(8,128)S(1)}, f32[16,10496]{1,0:T(8,128)}, u32[]{:S(2)}) copy-start(f32[16,10496]{1,0:T(8,128)} %param.21) | copy-start | bytes 2015236
  16.2 8.1 %copy-start.2 = (f32[16,10496]{1,0:T(8,128)S(1)}, f32[16,10496]{1,0:T(8,128)}, u32[]{:S(2)}) copy-start(f32[16,10496]{1,0:T(8,128)} %param.22) | copy-start | bytes 2015236
  18.4 15.2 %all-to-all-start.1 = ((bf16[16,2,5248]{2,1,0:T(2,128)(2,1)}), bf16[16,2,5248]{2,1,0:T(2,128)(2,1)S(1)}, u32[]{:S(2)}, u32[]{:S(2)}) async-start(bf16[16,2,5248]{2,1,0:T(2,128)(2,1)} %reshape.129), calls=%async_computation.1 | async-start | bytes 671744 | tf_op jit(solution)/shard_map/all_to_all | solution.py:680
  134.6 1.6 copy-start.3
  134.6 1.7 copy-start.5
  134.6 1.9 copy-start.4

commit v2 on v1

--- a/solution.py
+++ b/solution.py
@@ -65,26 +65,7 @@
     )
 
 
-def train_kernel(
-    tok,
-    cot,
-    weight,
-    wf,
-    wd,
-    a_in,
-    b_in,
-    a_out,
-    b_out,
-    out_a_in,
-    out_b_in,
-    out_a_out,
-    out_b_out,
-    held_tok,
-    held_cot,
-    send,
-    recv,
-):
-    devices = lax.axis_size("ep")
+def snake(devices):
     chips = devices // 2
     half = chips // 2
     me = lax.axis_index("ep")
@@ -96,56 +77,322 @@
         position = lax.rem(position + 2 * chips, chips)
         return jnp.where(position < half, 2 * position, 2 * (chips - 1 - position) + 1)
 
+    return me, core, chip, place, chip_at
+
+
+def spread(block):
+    pieces = []
+    for start in range(0, block.shape[0], 128):
+        cut = block[start : start + 128]
+        count = cut.shape[0]
+        shape = (4 * count, count)
+        rows = lax.broadcasted_iota(jnp.int32, shape, 0)
+        repeat = (rows // 4 == lax.broadcasted_iota(jnp.int32, shape, 1)).astype(jnp.bfloat16)
+        wide = product(repeat, cut)
+        shape = (4 * count, 128)
+        rows = lax.broadcasted_iota(jnp.int32, shape, 0)
+        lanes = lax.broadcasted_iota(jnp.int32, shape, 1)
+        wide = jnp.where(lanes // RANK == lax.rem(rows, 4), wide, 0.0).astype(jnp.bfloat16)
+        shape = (128, RANK)
+        lanes = lax.broadcasted_iota(jnp.int32, shape, 0)
+        fold = (lax.rem(lanes, RANK) == lax.broadcasted_iota(jnp.int32, shape, 1)).astype(
+            jnp.bfloat16
+        )
+        pieces.append(product(wide, fold).astype(jnp.bfloat16))
+    return jnp.concatenate(pieces, axis=0)
+
+
+def weave(block):
+    count = block.shape[0]
+    times = count // RANK
+    shape = (count, count)
+    rows = lax.broadcasted_iota(jnp.int32, shape, 0)
+    source = lax.rem(rows, RANK) * times + rows // RANK
+    pick = (source == lax.broadcasted_iota(jnp.int32, shape, 1)).astype(jnp.bfloat16)
+    sorted_rows = product(pick, block).astype(jnp.bfloat16)
+    return jnp.concatenate(
+        [sorted_rows[RANK * j : RANK * (j + 1)] for j in range(times)], axis=1
+    )
+
+
+def unspread(block):
+    pieces = []
+    for start in range(0, block.shape[1], 512):
+        cut = block[:, start : start + 512]
+        count = cut.shape[1]
+        shape = (RANK, 128)
+        rows = lax.broadcasted_iota(jnp.int32, shape, 0)
+        lanes = lax.broadcasted_iota(jnp.int32, shape, 1)
+        tile = (lax.rem(lanes, RANK) == rows).astype(jnp.bfloat16)
+        wide = outer(cut, tile)
+        shape = (count, 128)
+        rows = lax.broadcasted_iota(jnp.int32, shape, 0)
+        lanes = lax.broadcasted_iota(jnp.int32, shape, 1)
+        wide = jnp.where(lanes // RANK == lax.rem(rows, 4), wide, 0.0).astype(jnp.bfloat16)
+        shape = (count // 4, count)
+        rows = lax.broadcasted_iota(jnp.int32, shape, 0)
+        collapse = (rows == lax.broadcasted_iota(jnp.int32, shape, 1) // 4).astype(jnp.bfloat16)
+        pieces.append(product(collapse, wide))
+    return jnp.concatenate(pieces, axis=0)
+
+
+def unweave(block):
+    times = block.shape[1] // 128
+    stacked = jnp.concatenate([block[:, 128 * j : 128 * (j + 1)] for j in range(times)], axis=0)
+    shape = (RANK * times, RANK * times)
+    rows = lax.broadcasted_iota(jnp.int32, shape, 0)
+    source = lax.rem(rows, times) * RANK + rows // times
+    pick = (source == lax.broadcasted_iota(jnp.int32, shape, 1)).astype(jnp.bfloat16)
+    return product(pick, stacked)
+
+
+def flatten(gradients, flat, pieces):
+    start = 0
+    for grad, undo in zip(gradients, (unspread, unweave, unspread, unweave)):
+        rows = undo(grad[...].astype(jnp.bfloat16))
+        flat[start : start + rows.shape[0], :] = rows
+        start += rows.shape[0]
+    count = pieces.shape[1]
+    for j in range(pieces.shape[0]):
+        pieces[j] = flat[count * j : count * (j + 1), :].astype(jnp.bfloat16)
+
+
+def outer(left_op, right_op):
+    return lax.dot_general(
+        left_op, right_op, (((0,), (0,)), ((), ())), preferred_element_type=jnp.float32
+    )
+
+
+def times_transposed(left_op, right_op):
+    return lax.dot_general(
+        left_op, right_op, (((1,), (1,)), ((), ())), preferred_element_type=jnp.float32
+    )
+
+
+def column(row):
+    shape = (row.shape[1], row.shape[1])
+    same = lax.broadcasted_iota(jnp.int32, shape, 0) == lax.broadcasted_iota(jnp.int32, shape, 1)
+    return jnp.sum(jnp.where(same, row, 0.0), axis=1, keepdims=True)
+
+
+def restore(pieces, flat, factors):
+    count = pieces.shape[1]
+    for j in range(pieces.shape[0]):
+        flat[count * j : count * (j + 1), :] = pieces[j].astype(jnp.float32)
+    cuts = [0]
+    for size in (D * RANK, RANK * 2 * FF, FF * RANK, RANK * D):
+        cuts.append(cuts[-1] + size // 128)
+    for k, undo in enumerate((spread, weave, spread, weave)):
+        factors[k][...] = undo(flat[cuts[k] : cuts[k + 1], :].astype(jnp.bfloat16))
+
+
+def job_kernel(
+    owner,
+    held_by,
+    tok,
+    cot,
+    ids,
+    gains_in,
+    rows_in,
+    master,
+    moment_in,
+    second_in,
+    wf_in,
+    wd_in,
+    updated,
+    decoded,
+    wf,
+    wd,
+    moment,
+    second,
+    held_tok,
+    held_cot,
+    sent_gain,
+    gain,
+    sent_master,
+    got_master,
+    grads,
+    out_a_in,
+    out_b_in,
+    out_a_out,
+    out_b_out,
+    got_grads,
+    fresh,
+    serving,
+    pieces,
+    flat,
+    a_in,
+    b_in,
+    a_out,
+    b_out,
+    held,
+    base,
+    keep,
+    give,
+    got,
+    out_buf,
+    in_buf,
+    load_sem,
+    big_send,
+    big_recv,
+    gain_send,
+    gain_recv,
+    piece_send,
+    piece_recv,
+    row_send,
+    row_recv,
+    give_send,
+    give_recv,
+    sum_send,
+    sum_recv,
+):
+    devices = lax.axis_size("ep")
+    half = devices // 4
+    me, core, chip, place, chip_at = snake(devices)
     right = 2 * chip_at(place + 1) + core
     left = 2 * chip_at(place - 1) + core
     sibling = 2 * chip + 1 - core
-    held = (held_tok, held_cot)
-
+    count = rows_in.shape[0]
+    part = count // 2
+
+    loads = [
+        pltpu.make_async_copy(source, target, load_sem.at[k])
+        for k, (source, target) in enumerate(
+            ((wf_in, wf), (wd_in, wd), (moment_in, moment), (second_in, second))
+        )
+    ]
+    for load in loads:
+        load.start()
+    bigs = (held_tok, held_cot)
     barrier = pltpu.get_barrier_semaphore()
-    for other in (left, right, sibling):
+
+    def greet(k, carry):
         pl.semaphore_signal(
-            barrier, inc=1, device_id={"ep": other}, device_id_type=pl.DeviceIdType.MESH
-        )
-    pl.semaphore_wait(barrier, 3)
-
-    def move(kind, source, slot, other):
+            barrier,
+            inc=1,
+            device_id={"ep": lax.rem(me + k, devices)},
+            device_id_type=pl.DeviceIdType.MESH,
+        )
+        return carry
+
+    lax.fori_loop(1, devices, greet, 0)
+    pl.semaphore_wait(barrier, devices - 1)
+
+    def remote(source, target, send, recv, other):
         return pltpu.make_async_remote_copy(
             src_ref=source,
-            dst_ref=held[kind].at[slot],
-            send_sem=send.at[kind, slot],
-            recv_sem=recv.at[kind, slot],
+            dst_ref=target,
+            send_sem=send,
+            recv_sem=recv,
             device_id={"ep": other},
             device_id_type=pl.DeviceIdType.MESH,
         )
 
+    def big_move(kind, source, slot, other):
+        return remote(
+            source, bigs[kind].at[slot], big_send.at[kind, slot], big_recv.at[kind, slot], other
+        )
+
+    def big_arrived(kind, slot):
+        big_move(kind, bigs[kind].at[slot], slot, sibling).wait_recv()
+
     for kind, own in ((0, tok), (1, cot)):
-        move(kind, own, 2, right).start()
-        move(kind, own, 3, left).start()
-        move(kind, own, 1, sibling).start()
+        big_move(kind, own, 2, right).start()
+        big_move(kind, own, 3, left).start()
+        big_move(kind, own, 1, sibling).start()
+
+    def piece_to(kind, source, target, other):
+        return remote(
+            source.at[other],
+            target.at[me],
+            piece_send.at[kind, other],
+            piece_recv.at[kind, me],
+            other,
+        )
+
+    def piece_from(kind, source, target, other):
+        return remote(
+            source.at[other],
+            target.at[other],
+            piece_send.at[kind, other],
+            piece_recv.at[kind, other],
+            other,
+        )
+
+    def each_other(act):
+        def body(k, carry):
+            act(lax.rem(me + k, devices))
+            return carry
+
+        lax.fori_loop(1, devices, body, 0)
+
+    def gain_to(other):
+        return remote(
+            sent_gain.at[other], gain.at[me], gain_send.at[other], gain_recv.at[me], other
+        )
+
+    def gain_from(other):
+        return remote(
+            sent_gain.at[other], gain.at[other], gain_send.at[other], gain_recv.at[other], other
+        )
+
+    def hand_out(k, carry):
+        other = lax.rem(me + k, devices)
+        expert = held_by[other]
+        sent_master[other] = master[expert].astype(jnp.bfloat16)
+        named = jnp.sum(
+            jnp.where(ids[...] == expert, gains_in[...], 0.0), axis=0, keepdims=True
+        )
+        sent_gain[other] = jnp.broadcast_to(named, sent_gain.shape[1:])
+
+        @pl.when(k < devices)
+        def _():
+            piece_to(2, sent_master, got_master, other).start()
+            gain_to(other).start()
+
+        return carry
+
+    lax.fori_loop(1, devices + 1, hand_out, 0)
+    got_master[me] = sent_master[me]
+    gain[me] = sent_gain[me]
     held_tok[0] = tok[...]
     held_cot[0] = cot[...]
-    for out in (out_a_in, out_b_in, out_a_out, out_b_out):
+    gradients = (out_a_in, out_b_in, out_a_out, out_b_out)
+    for out in gradients:
         out[...] = jnp.zeros_like(out)
-
-    def arrived(kind, slot):
-        move(kind, held[kind].at[slot], slot, sibling).wait_recv()
-
-    def outer(left_op, right_op):
-        return lax.dot_general(
-            left_op, right_op, (((0,), (0,)), ((), ())), preferred_element_type=jnp.float32
-        )
-
-    def times_transposed(left_op, right_op):
-        return lax.dot_general(
-            left_op, right_op, (((1,), (1,)), ((), ())), preferred_element_type=jnp.float32
-        )
+    each_other(lambda other: piece_from(2, sent_master, got_master, other).wait_recv())
+    each_other(lambda other: gain_from(other).wait_recv())
+    restore(got_master, flat, (a_in, b_in, a_out, b_out))
+    loads[0].wait()
+    loads[1].wait()
+
+    def cut(slot, kind):
+        return held.at[slot, pl.ds(part * kind, part)]
+
+    def row_move(source, slot, kind, other):
+        return remote(
+            source, cut(slot, kind), row_send.at[kind, slot], row_recv.at[kind, slot], other
+        )
+
+    def row_arrived(slot, kind):
+        row_move(cut(slot, kind), slot, kind, sibling).wait_recv()
+
+    def gain_of(source, start, size):
+        return column(gain[source][0:1, start : start + size])
+
+    def start_rows():
+        for kind in (0, 1):
+            own = rows_in.at[pl.ds(part * kind, part)]
+            row_move(own, 4, kind, right).start()
+            row_move(own, 5, kind, left).start()
+            row_move(own, 2, kind, sibling).start()
 
     def learn(tile, first, second):
         count, width = tok.shape
         pair = pl.ds(2 * tile, 2)
         rows = held_tok[pair].reshape(2 * count, width)
-        gain = jnp.concatenate([weight[first], weight[second]], axis=0)
-        grad = (gain * held_cot[pair].reshape(2 * count, width).astype(jnp.float32)).astype(
+        gains = jnp.concatenate([gain_of(first, 0, count), gain_of(second, 0, count)], axis=0)
+        grad = (gains * held_cot[pair].reshape(2 * count, width).astype(jnp.float32)).astype(
             jnp.bfloat16
         )
         mid_in = product(rows, a_in[...]).astype(jnp.bfloat16)
@@ -170,42 +417,47 @@
         out_a_in[...] += outer(back_in, rows)
 
     def step(s, carry):
-        base = 4 * s - 2
+        slot0 = 4 * s - 2
 
         @pl.when(s == 0)
         def _():
             for kind in (0, 1):
-                arrived(kind, 1)
+                big_arrived(kind, 1)
 
         @pl.when((s > 0) & (s < half))
         def _():
             for kind in (0, 1):
                 for way, onward in ((0, right), (1, left)):
-                    slot = base + way
-                    arrived(kind, slot)
+                    slot = slot0 + way
+                    big_arrived(kind, slot)
 
                     @pl.when(s < half - 1)
                     def _():
-                        move(kind, held[kind].at[slot], slot + 4, onward).start()
+                        big_move(kind, bigs[kind].at[slot], slot + 4, onward).start()
 
                     if way == kind:
 
                         @pl.when(s == half - 1)
                         def _():
-                            move(kind, held[kind].at[slot], 4 * half - 2, onward).start()
-
-                    move(kind, held[kind].at[slot], slot + 2, sibling).start()
+                            big_move(kind, bigs[kind].at[slot], 4 * half - 2, onward).start()
+
+                    big_move(kind, bigs[kind].at[slot], slot + 2, sibling).start()
+
+            @pl.when(s == half - 1)
+            def _():
+                start_rows()
+
             for kind in (0, 1):
                 for way in (0, 1):
-                    arrived(kind, base + 2 + way)
+                    big_arrived(kind, slot0 + 2 + way)
 
         @pl.when(s == half)
         def _():
             for kind in (0, 1):
-                arrived(kind, base)
-                move(kind, held[kind].at[base], base + 1, sibling).start()
+                big_arrived(kind, slot0)
+                big_move(kind, bigs[kind].at[slot0], slot0 + 1, sibling).start()
             for kind in (0, 1):
-                arrived(kind, base + 1)
+                big_arrived(kind, slot0 + 1)
 
         single = (s == 0) | (s == half)
         from_left = 2 * chip_at(place - s)
@@ -222,218 +474,32 @@
 
     lax.fori_loop(0, half + 1, step, 0)
 
-    def sent(slot, carry):
-        for kind in (0, 1):
-            move(kind, held[kind].at[slot], slot, sibling).wait_send()
-        return carry
-
-    lax.fori_loop(1, devices, sent, 0)
-
-
-def train(tokens, cotangent, weight, joined_weight, down_weight, flat_bf):
-    devices = lax.axis_size("ep")
-    count, width = tokens.shape
-    a_in, b_in, a_out, b_out = unpack(flat_bf)
-    shape = lambda *size: jax.ShapeDtypeStruct(size, jnp.float32)
-    vmem = pl.BlockSpec(memory_space=pltpu.VMEM)
-    g_a_in, g_b_in, g_a_out, g_b_out = pl.pallas_call(
-        train_kernel,
-        out_shape=(shape(RANK, width), shape(RANK, 2 * FF), shape(RANK, FF), shape(RANK, width)),
-        in_specs=[vmem] * 9,
-        out_specs=(vmem,) * 4,
-        scratch_shapes=[
-            pltpu.VMEM((devices, count, width), jnp.bfloat16),
-            pltpu.VMEM((devices, count, width), jnp.bfloat16),
-            pltpu.SemaphoreType.DMA((2, devices)),
-            pltpu.SemaphoreType.DMA((2, devices)),
-        ],
-        compiler_params=pltpu.CompilerParams(
-            collective_id=0, has_side_effects=True, vmem_limit_bytes=56 * 1024 * 1024
-        ),
-        name="train",
-    )(tokens, cotangent, weight, joined_weight, down_weight, a_in, b_in, a_out, b_out)
-    return jnp.concatenate(
-        [g_a_in.T.reshape(-1), g_b_in.reshape(-1), g_a_out.T.reshape(-1), g_b_out.reshape(-1)]
-    )
-
-
-def snake(devices):
-    chips = devices // 2
-    half = chips // 2
-    me = lax.axis_index("ep")
-    core = lax.rem(me, 2)
-    chip = me // 2
-    place = jnp.where(lax.rem(chip, 2) == 0, chip // 2, chips - 1 - chip // 2)
-
-    def chip_at(position):
-        position = lax.rem(position + 2 * chips, chips)
-        return jnp.where(position < half, 2 * position, 2 * (chips - 1 - position) + 1)
-
-    return me, core, chip, place, chip_at
-
-
-def spread(block):
-    pieces = []
-    for start in range(0, block.shape[0], 128):
-        cut = block[start : start + 128]
-        count = cut.shape[0]
-        shape = (4 * count, count)
-        rows = lax.broadcasted_iota(jnp.int32, shape, 0)
-        repeat = (rows // 4 == lax.broadcasted_iota(jnp.int32, shape, 1)).astype(jnp.bfloat16)
-        wide = product(repeat, cut)
-        shape = (4 * count, 128)
-        rows = lax.broadcasted_iota(jnp.int32, shape, 0)
-        lanes = lax.broadcasted_iota(jnp.int32, shape, 1)
-        wide = jnp.where(lanes // RANK == lax.rem(rows, 4), wide, 0.0).astype(jnp.bfloat16)
-        shape = (128, RANK)
-        lanes = lax.broadcasted_iota(jnp.int32, shape, 0)
-        fold = (lax.rem(lanes, RANK) == lax.broadcasted_iota(jnp.int32, shape, 1)).astype(
-            jnp.bfloat16
-        )
-        pieces.append(product(wide, fold).astype(jnp.bfloat16))
-    return jnp.concatenate(pieces, axis=0)
-
-
-def weave(block):
-    count = block.shape[0]
-    times = count // RANK
-    shape = (count, count)
-    rows = lax.broadcasted_iota(jnp.int32, shape, 0)
-    source = lax.rem(rows, RANK) * times + rows // RANK
-    pick = (source == lax.broadcasted_iota(jnp.int32, shape, 1)).astype(jnp.bfloat16)
-    sorted_rows = product(pick, block).astype(jnp.bfloat16)
-    return jnp.concatenate(
-        [sorted_rows[RANK * j : RANK * (j + 1)] for j in range(times)], axis=1
-    )
-
-
-def restore(pieces, flat, factors):
-    count = pieces.shape[1]
-    for j in range(pieces.shape[0]):
-        flat[count * j : count * (j + 1), :] = pieces[j].astype(jnp.float32)
-    cuts = [0]
-    for size in (D * RANK, RANK * 2 * FF, FF * RANK, RANK * D):
-        cuts.append(cuts[-1] + size // 128)
-    for k, undo in enumerate((spread, weave, spread, weave)):
-        factors[k][...] = undo(flat[cuts[k] : cuts[k + 1], :].astype(jnp.bfloat16))
-
-
-def serve_kernel(
-    owner,
-    held_by,
-    grads,
-    master,
-    moment,
-    second,
-    rows_in,
-    weight,
-    wf,
-    wd,
-    updated,
-    decoded,
-    got_grads,
-    fresh,
-    serving,
-    pieces,
-    flat,
-    a_in,
-    b_in,
-    a_out,
-    b_out,
-    held,
-    base,
-    keep,
-    give,
-    got,
-    out_buf,
-    in_buf,
-    piece_send,
-    piece_recv,
-    row_send,
-    row_recv,
-    give_send,
-    give_recv,
-    sum_send,
-    sum_recv,
-):
-    devices = lax.axis_size("ep")
-    half = devices // 4
-    me, core, chip, place, chip_at = snake(devices)
-    right = 2 * chip_at(place + 1) + core
-    left = 2 * chip_at(place - 1) + core
-    sibling = 2 * chip + 1 - core
-    count = rows_in.shape[0]
-    part = count // 2
-
-    barrier = pltpu.get_barrier_semaphore()
-
-    def greet(k, carry):
-        pl.semaphore_signal(
-            barrier,
-            inc=1,
-            device_id={"ep": lax.rem(me + k, devices)},
-            device_id_type=pl.DeviceIdType.MESH,
-        )
-        return carry
-
-    lax.fori_loop(1, devices, greet, 0)
-    pl.semaphore_wait(barrier, devices - 1)
-
-    def remote(source, target, send, recv, other):
-        return pltpu.make_async_remote_copy(
-            src_ref=source,
-            dst_ref=target,
-            send_sem=send,
-            recv_sem=recv,
-            device_id={"ep": other},
-            device_id_type=pl.DeviceIdType.MESH,
-        )
-
-    def piece_to(kind, source, target, other):
-        return remote(
-            source.at[other],
-            target.at[me],
-            piece_send.at[kind, other],
-            piece_recv.at[kind, me],
-            other,
-        )
-
-    def piece_from(kind, source, target, other):
-        return remote(
-            source.at[other],
-            target.at[other],
-            piece_send.at[kind, other],
-            piece_recv.at[kind, other],
-            other,
-        )
-
-    def each_other(act):
-        def body(k, carry):
-            act(lax.rem(me + k, devices))
-            return carry
-
-        lax.fori_loop(1, devices, body, 0)
-
+    flatten(gradients, flat, grads)
     each_other(lambda other: piece_to(0, grads, got_grads, other).start())
-
-    def cut(slot, kind):
-        return held.at[slot, pl.ds(part * kind, part)]
-
-    def row_move(source, slot, kind, other):
-        return remote(
-            source, cut(slot, kind), row_send.at[kind, slot], row_recv.at[kind, slot], other
-        )
-
-    def row_arrived(slot, kind):
-        row_move(cut(slot, kind), slot, kind, sibling).wait_recv()
-
-    for kind in (0, 1):
-        own = rows_in.at[pl.ds(part * kind, part)]
-        row_move(own, 4, kind, right).start()
-        row_move(own, 5, kind, left).start()
-        row_move(own, 2, kind, sibling).start()
     held[0] = rows_in[...]
     got_grads[me] = grads[me]
+    def row_step(s, carry):
+        for kind in (0, 1):
+            for way, onward in ((0, right), (1, left)):
+                slot = 4 * s + way
+                row_arrived(slot, kind)
+
+                @pl.when(s < half - 1)
+                def _():
+                    row_move(cut(slot, kind), slot + 4, kind, onward).start()
+
+                if way == kind:
+
+                    @pl.when(s == half - 1)
+                    def _():
+                        row_move(cut(slot, kind), 1, kind, onward).start()
+
+                row_move(cut(slot, kind), slot + 2, kind, sibling).start()
+        return carry
+
+    lax.fori_loop(1, half - 1, row_step, 0)
+    loads[2].wait()
+    loads[3].wait()
     each_other(lambda other: piece_from(0, grads, got_grads, other).wait_recv())
 
     def renew(k, carry):
@@ -453,26 +519,7 @@
     lax.fori_loop(1, devices + 1, renew, 0)
     pieces[me] = serving[me]
 
-    def row_step(s, carry):
-        for kind in (0, 1):
-            for way, onward in ((0, right), (1, left)):
-                slot = 4 * s + way
-                row_arrived(slot, kind)
-
-                @pl.when(s < half - 1)
-                def _():
-                    row_move(cut(slot, kind), slot + 4, kind, onward).start()
-
-                if way == kind:
-
-                    @pl.when(s == half - 1)
-                    def _():
-                        row_move(cut(slot, kind), 1, kind, onward).start()
-
-                row_move(cut(slot, kind), slot + 2, kind, sibling).start()
-        return carry
-
-    lax.fori_loop(1, half, row_step, 0)
+    lax.fori_loop(half - 1, half, row_step, 0)
 
     def write_back(expert, carry):
         updated[expert] = fresh[owner[expert]]
@@ -516,10 +563,10 @@
         second_chip = 2 * chip_at(place + jnp.where(s == 0, half, s))
         gains = jnp.concatenate(
             [
-                weight[first + core],
-                weight[second_chip + core],
-                weight[first + 1 - core],
-                weight[second_chip + 1 - core],
+                gain_of(first + core, tok.shape[0], count),
+                gain_of(second_chip + core, tok.shape[0], count),
+                gain_of(first + 1 - core, tok.shape[0], count),
+                gain_of(second_chip + 1 - core, tok.shape[0], count),
             ],
             axis=0,
         )
@@ -575,12 +622,15 @@
     def piece_sent(other):
         piece_to(0, grads, got_grads, other).wait_send()
         piece_to(1, serving, pieces, other).wait_send()
+        piece_to(2, sent_master, got_master, other).wait_send()
+        gain_to(other).wait_send()
 
     each_other(piece_sent)
 
     def rows_sent(slot, carry):
         for kind in (0, 1):
             row_move(cut(slot, kind), slot, kind, sibling).wait_send()
+            big_move(kind, bigs[kind].at[slot], slot, sibling).wait_send()
         return carry
 
     lax.fori_loop(1, devices, rows_sent, 0)
@@ -593,21 +643,39 @@
                     sum_move(way, t, piece, left).wait_send()
 
 
-def serve(owner, held_by, grads, master, moment, second, rows, weight, joined_weight, down_weight):
+def job(owner, held_by, tokens, cotangent, ids, gains, rows, master, moment, second, wf, wd):
     devices = lax.axis_size("ep")
     half = devices // 4
     count, width = rows.shape
     lane_rows = master.shape[1] // 128
     cube = (devices, lane_rows, 128)
+    blocks = (devices,) + tokens.shape
     vmem = pl.BlockSpec(memory_space=pltpu.VMEM)
     smem = pl.BlockSpec(memory_space=pltpu.SMEM)
+    anywhere = pl.BlockSpec(memory_space=pl.ANY)
     bf, f32 = jnp.bfloat16, jnp.float32
+    sems = pltpu.SemaphoreType.DMA
     updated, decoded = pl.pallas_call(
-        serve_kernel,
+        job_kernel,
         out_shape=(jax.ShapeDtypeStruct(cube, f32), jax.ShapeDtypeStruct((count, width), bf)),
-        in_specs=[smem] * 2 + [vmem] * 8,
+        in_specs=[smem] * 2 + [vmem] * 6 + [anywhere] * 4,
         out_specs=(vmem,) * 2,
         scratch_shapes=[
+            pltpu.VMEM(wf.shape, bf),
+            pltpu.VMEM(wd.shape, bf),
+            pltpu.VMEM(cube, f32),
+            pltpu.VMEM(cube, f32),
+            pltpu.VMEM(blocks, bf),
+            pltpu.VMEM(blocks, bf),
+            pltpu.VMEM((devices,) + gains.shape, f32),
+            pltpu.VMEM((devices,) + gains.shape, f32),
+            pltpu.VMEM(cube, bf),
+            pltpu.VMEM(cube, bf),
+            pltpu.VMEM(cube, bf),
+            pltpu.VMEM((RANK, width), f32),
+            pltpu.VMEM((RANK, 2 * FF), f32),
+            pltpu.VMEM((RANK, FF), f32),
+            pltpu.VMEM((RANK, width), f32),
             pltpu.VMEM(cube, bf),
             pltpu.VMEM(cube, f32),
             pltpu.VMEM(cube, bf),
@@ -624,30 +692,37 @@
             pltpu.VMEM((half, 2, count, width), bf),
             pltpu.VMEM((2, half, count, width), bf),
             pltpu.VMEM((2, half, count, width), bf),
-            pltpu.SemaphoreType.DMA((2, devices)),
-            pltpu.SemaphoreType.DMA((2, devices)),
-            pltpu.SemaphoreType.DMA((2, devices)),
-            pltpu.SemaphoreType.DMA((2, devices)),
-            pltpu.SemaphoreType.DMA((half,)),
-            pltpu.SemaphoreType.DMA((half,)),
-            pltpu.SemaphoreType.DMA((2, half, 2)),
-            pltpu.SemaphoreType.DMA((2, half, 2)),
+            sems((4,)),
+            sems((2, devices)),
+            sems((2, devices)),
+            sems((devices,)),
+            sems((devices,)),
+            sems((3, devices)),
+            sems((3, devices)),
+            sems((2, devices)),
+            sems((2, devices)),
+            sems((half,)),
+            sems((half,)),
+            sems((2, half, 2)),
+            sems((2, half, 2)),
         ],
         compiler_params=pltpu.CompilerParams(
-            collective_id=1, has_side_effects=True, vmem_limit_bytes=56 * 1024 * 1024
+            collective_id=0, has_side_effects=True, vmem_limit_bytes=60 * 1024 * 1024
         ),
-        name="serve",
+        name="job",
     )(
         owner,
         held_by,
-        grads.astype(bf).reshape(cube),
+        tokens,
+        cotangent,
+        ids,
+        gains,
+        rows,
         master.reshape(cube),
         moment.reshape(cube),
         second.reshape(cube),
-        rows,
-        weight,
-        joined_weight,
-        down_weight,
+        wf,
+        wd,
     )
     return updated.reshape(master.shape), decoded
 
@@ -704,6 +779,29 @@
     held_by = jnp.sum(jnp.where(owner[None, :] == labels[:, None], labels[None, :], 0), axis=1)
     steps, dec_rows = step_rows.shape[:2]
 
+    tok_rows = tokens.shape[0]
+    flat_rows = step_rows.reshape(steps * dec_rows, width)
+    if experts == 16:
+        def to_lanes(first, last):
+            both = jnp.concatenate([first, last.reshape(steps * dec_rows, -1)]).T
+            return jnp.pad(both, ((0, 0), (0, -both.shape[1] % 128)))
+
+        updated, decoded = job(
+            owner,
+            held_by,
+            tokens,
+            cotangent,
+            to_lanes(route_ids, step_ids),
+            to_lanes(route_weights, step_weights),
+            flat_rows,
+            master,
+            moment,
+            second,
+            joined_weight,
+            down_weight,
+        )
+        return (updated, decoded.reshape(steps, dec_rows, width))
+
     def gather(array):
         return lax.all_gather(array, "ep", axis=0, tiled=True)
 
@@ -718,32 +816,9 @@
         ]
     )
     all_weights = exchange(my_weights.T[:, None, :])[:, 0, :]
-    tok_rows = tokens.shape[0]
     chunks = max(1, experts // 16)
     part = tok_rows // chunks
     flat_bf = exchange(jnp.take(master.astype(jnp.bfloat16), held_by, axis=0)).reshape(-1)
-    if experts == 16:
-        grads = train(
-            tokens,
-            cotangent,
-            all_weights[:, :tok_rows, None],
-            joined_weight,
-            down_weight,
-            flat_bf,
-        )
-        updated, decoded = serve(
-            owner,
-            held_by,
-            grads,
-            master,
-            moment,
-            second,
-            step_rows.reshape(steps * dec_rows, width),
-            all_weights[:, tok_rows:, None],
-            joined_weight,
-            down_weight,
-        )
-        return (updated, decoded.reshape(steps, dec_rows, width))
     grads = 0.0
     for chunk in range(chunks):
         cut = slice(chunk * part, (chunk + 1) * part)

time: 205 us -> 183 us (0.89)
  starting transfers between devices: 11.4 us -> 0 us
  Pallas kernels: 157 us -> 168 us
  local copies, waits for them, and re-layouts: 19.9 us -> 11.5 us
  waiting for transfers between devices: 8.19 us -> 0 us
  other arithmetic: 6.98 us -> 2.8 us
    all_to_all x2 -> x0, starting transfers between devices: 11.4 us -> none  [exchange(): return lax.all_to_all(array, 'ep', split_axis=0, concat_axis=0, tiled=True)]
    pallas_call x2 -> x1, Pallas kernels: 157 us -> 168 us  [job(): pl.pallas_call(job_kernel, out_shape=(jax.ShapeDtypeStruct(cube, f32), ja...]
    all_to_all x2 -> x0, waiting for transfers between devices: 8.19 us -> none  [exchange(): return lax.all_to_all(array, 'ep', split_axis=0, concat_axis=0, tiled=True)]
    broadcast_in_dim x6 -> x0, local copies, waits for them, and re-layouts: 3.65 us -> none  [the longest x2 1.37 us: on_device(): all_weights[:, :tok_rows, None]]
    slice x6 -> x0, local copies, waits for them, and re-layouts: 3.52 us -> none  [the longest x2 1.74 us: unpack(): a_in = flat[:cut_one].reshape(D, RANK)]
    all_to_all x1 -> x0, other arithmetic: 2.08 us -> none  [exchange(): return lax.all_to_all(array, 'ep', split_axis=0, concat_axis=0, tiled=True)]
    reshape x8 -> x5, local copies, waits for them, and re-layouts: 4.62 us -> 6.65 us  [the longest x1 2.06 us: job(): moment.reshape(cube)]
    unnamed x20 -> x4, local copies, waits for them, and re-layouts: 4.79 us -> 3.65 us
  transfers between devices with their start and end apart: 2 -> 0, of which waited for: 2 -> 0; matrix products, arithmetic and copies ran while one was open for 5% -> 0% of each run, Pallas kernels for 0% -> 0%
where the time goes in v2:
time: 183 us; the launch traced here: 182 us
  Pallas kernels  168 us (92%)
  local copies, waits for them, and re-layouts  11.5 us (6%)
  other arithmetic  2.8 us (2%)
    pallas_call x1, Pallas kernels, job(): pl.pallas_call(job_kernel, out_shape=(jax.ShapeDtypeStruct(cube, f32), ja...  168 us

profile of v2, /device:TPU:0, one launch (start us, length us, event | category | flops | bytes accessed | tf_op | source)
XLA Modules:
  0.0 182.5 jit_solution(10701539310884237933)
XLA Ops:
  0.6 0.0 copy-start
  0.6 1.4 select_reduce_fusion.held_by
  2.0 0.8 copy.21
  2.8 0.7 add_bitcast_fusion
  3.5 0.6 pad.8.ids
  4.1 0.8 copy.22
  4.9 0.7 maximum_bitcast_fusion
  5.6 0.6 pad.9.gains_in
  6.2 2.0 %reshape.32.master = f32[16,82,128]{2,1,0:T(8,128)} reshape(f32[16,10496]{1,0:T(8,128)} %param.20) | data formatting | bytes 1343488 | tf_op jit(solution)/shard_map/reshape | solution.py:721
  8.3 2.1 %reshape.33.moment_in = f32[16,82,128]{2,1,0:T(8,128)} reshape(f32[16,10496]{1,0:T(8,128)} %param.21) | data formatting | bytes 1343488 | tf_op jit(solution)/shard_map/reshape | solution.py:722
  10.3 0.0 copy-done
  10.3 1.0 reshape.34.second_in
  11.3 167.5 %job.1 = (f32[16,82,128]{2,1,0:T(8,128)}, bf16[32,2048]{1,0:T(8,128)(2,1)}) custom-call(s32[16]{0:T(128)} %owner.1, s32[16]{0:T(128)} %select_reduce_fusion.held_by, bf16[128,2048]{1,0:T(8,128)(2,1)} %tok.1, bf16[128,2048]{1,0:T(8,128)(2,1)} %cot.1, s32[8,256]{1,0:T(8,128)} %pad.8.ids, f32[8,256]{1,0:T(8,128)} %pad.9.gains_in, bf16[32,2048]{1,0:T(8,128)(2,1)} %bitcast.18, ...), custom_call_target="tpu_custom_call" | custom-call | tf_op jit(solution)/shard_map/job/pallas_call | solution.py:658
  178.8 2.1 %copy.25 = f32[2,8,82,128]{3,1,2,0:T(8,128)} copy(f32[2,8,82,128]{3,2,1,0:T(8,128)} %bitcast.16) | data formatting | bytes 1343488
  180.9 1.6 copy.27
Async XLA Ops:
  0.6 9.7 %copy-start = (f32[16,10496]{1,0:T(8,128)S(1)}, f32[16,10496]{1,0:T(8,128)}, u32[]{:S(2)}) copy-start(f32[16,10496]{1,0:T(8,128)} %param.22) | copy-start | bytes 2015236

commit v3 on v2

--- a/solution.py
+++ b/solution.py
@@ -87,15 +87,15 @@
         count = cut.shape[0]
         shape = (4 * count, count)
         rows = lax.broadcasted_iota(jnp.int32, shape, 0)
-        repeat = (rows // 4 == lax.broadcasted_iota(jnp.int32, shape, 1)).astype(jnp.bfloat16)
+        repeat = (rows >> 2 == lax.broadcasted_iota(jnp.int32, shape, 1)).astype(jnp.bfloat16)
         wide = product(repeat, cut)
         shape = (4 * count, 128)
         rows = lax.broadcasted_iota(jnp.int32, shape, 0)
         lanes = lax.broadcasted_iota(jnp.int32, shape, 1)
-        wide = jnp.where(lanes // RANK == lax.rem(rows, 4), wide, 0.0).astype(jnp.bfloat16)
+        wide = jnp.where(lanes >> 5 == rows & 3, wide, 0.0).astype(jnp.bfloat16)
         shape = (128, RANK)
         lanes = lax.broadcasted_iota(jnp.int32, shape, 0)
-        fold = (lax.rem(lanes, RANK) == lax.broadcasted_iota(jnp.int32, shape, 1)).astype(
+        fold = (lanes & (RANK - 1) == lax.broadcasted_iota(jnp.int32, shape, 1)).astype(
             jnp.bfloat16
         )
         pieces.append(product(wide, fold).astype(jnp.bfloat16))
@@ -107,7 +107,7 @@
     times = count // RANK
     shape = (count, count)
     rows = lax.broadcasted_iota(jnp.int32, shape, 0)
-    source = lax.rem(rows, RANK) * times + rows // RANK
+    source = (rows & (RANK - 1)) * times + (rows >> 5)
     pick = (source == lax.broadcasted_iota(jnp.int32, shape, 1)).astype(jnp.bfloat16)
     sorted_rows = product(pick, block).astype(jnp.bfloat16)
     return jnp.concatenate(
@@ -123,15 +123,15 @@
         shape = (RANK, 128)
         rows = lax.broadcasted_iota(jnp.int32, shape, 0)
         lanes = lax.broadcasted_iota(jnp.int32, shape, 1)
-        tile = (lax.rem(lanes, RANK) == rows).astype(jnp.bfloat16)
+        tile = (lanes & (RANK - 1) == rows).astype(jnp.bfloat16)
         wide = outer(cut, tile)
         shape = (count, 128)
         rows = lax.broadcasted_iota(jnp.int32, shape, 0)
         lanes = lax.broadcasted_iota(jnp.int32, shape, 1)
-        wide = jnp.where(lanes // RANK == lax.rem(rows, 4), wide, 0.0).astype(jnp.bfloat16)
+        wide = jnp.where(lanes >> 5 == rows & 3, wide, 0.0).astype(jnp.bfloat16)
         shape = (count // 4, count)
         rows = lax.broadcasted_iota(jnp.int32, shape, 0)
-        collapse = (rows == lax.broadcasted_iota(jnp.int32, shape, 1) // 4).astype(jnp.bfloat16)
+        collapse = (rows == lax.broadcasted_iota(jnp.int32, shape, 1) >> 2).astype(jnp.bfloat16)
         pieces.append(product(collapse, wide))
     return jnp.concatenate(pieces, axis=0)
 
@@ -140,9 +140,9 @@
     times = block.shape[1] // 128
     stacked = jnp.concatenate([block[:, 128 * j : 128 * (j + 1)] for j in range(times)], axis=0)
     shape = (RANK * times, RANK * times)
-    rows = lax.broadcasted_iota(jnp.int32, shape, 0)
-    source = lax.rem(rows, times) * RANK + rows // times
-    pick = (source == lax.broadcasted_iota(jnp.int32, shape, 1)).astype(jnp.bfloat16)
+    stack = lax.broadcasted_iota(jnp.int32, shape, 1)
+    target = (stack & (RANK - 1)) * times + (stack >> 5)
+    pick = (target == lax.broadcasted_iota(jnp.int32, shape, 0)).astype(jnp.bfloat16)
     return product(pick, stacked)
 
 
@@ -175,6 +175,16 @@
     return jnp.sum(jnp.where(same, row, 0.0), axis=1, keepdims=True)
 
 
+def to_cube(table, cube):
+    for j in range(cube.shape[1]):
+        cube[:, j, :] = table[:, 128 * j : 128 * (j + 1)]
+
+
+def to_table(cube, table):
+    for j in range(cube.shape[1]):
+        table[:, 128 * j : 128 * (j + 1)] = cube[:, j, :]
+
+
 def restore(pieces, flat, factors):
     count = pieces.shape[1]
     for j in range(pieces.shape[0]):
@@ -194,7 +204,7 @@
     ids,
     gains_in,
     rows_in,
-    master,
+    master_in,
     moment_in,
     second_in,
     wf_in,
@@ -203,6 +213,9 @@
     decoded,
     wf,
     wd,
+    moment_table,
+    second_table,
+    master,
     moment,
     second,
     held_tok,
@@ -258,7 +271,7 @@
     loads = [
         pltpu.make_async_copy(source, target, load_sem.at[k])
         for k, (source, target) in enumerate(
-            ((wf_in, wf), (wd_in, wd), (moment_in, moment), (second_in, second))
+            ((wf_in, wf), (wd_in, wd), (moment_in, moment_table), (second_in, second_table))
         )
     ]
     for load in loads:
@@ -335,6 +348,8 @@
         return remote(
             sent_gain.at[other], gain.at[other], gain_send.at[other], gain_recv.at[other], other
         )
+
+    to_cube(master_in, master)
 
     def hand_out(k, carry):
         other = lax.rem(me + k, devices)
@@ -443,6 +458,13 @@
 
                     big_move(kind, bigs[kind].at[slot], slot + 2, sibling).start()
 
+            @pl.when(s == 1)
+            def _():
+                loads[2].wait()
+                loads[3].wait()
+                to_cube(moment_table, moment)
+                to_cube(second_table, second)
+
             @pl.when(s == half - 1)
             def _():
                 start_rows()
@@ -498,8 +520,6 @@
         return carry
 
     lax.fori_loop(1, half - 1, row_step, 0)
-    loads[2].wait()
-    loads[3].wait()
     each_other(lambda other: piece_from(0, grads, got_grads, other).wait_recv())
 
     def renew(k, carry):
@@ -522,10 +542,11 @@
     lax.fori_loop(half - 1, half, row_step, 0)
 
     def write_back(expert, carry):
-        updated[expert] = fresh[owner[expert]]
+        master[expert] = fresh[owner[expert]]
         return carry
 
     lax.fori_loop(0, devices, write_back, 0)
+    to_table(master, updated)
     for kind in (0, 1):
         row_arrived(1, kind)
         row_move(cut(1, kind), 3, kind, sibling).start()
@@ -576,7 +597,7 @@
         remote(give.at[s], got.at[s], give_send.at[s], give_recv.at[s], sibling).start()
         return carry
 
-    lax.fori_loop(0, half, answer, 0)
+    lax.fori_loop(0, 2, answer, 0)
 
     def sum_move(way, t, piece, other):
         spot = pl.ds(part * piece, part)
@@ -601,6 +622,8 @@
         sum_move(way, 0, way, onward).start()
     for t in range(1, half):
         s = half - t
+        if t > 1:
+            lax.fori_loop(t, t + 1, answer, 0)
         got_wait(s)
         for way, onward in ((0, right), (1, left)):
             total = of_chip(s, 1 - way)
@@ -657,12 +680,15 @@
     sems = pltpu.SemaphoreType.DMA
     updated, decoded = pl.pallas_call(
         job_kernel,
-        out_shape=(jax.ShapeDtypeStruct(cube, f32), jax.ShapeDtypeStruct((count, width), bf)),
+        out_shape=(jax.ShapeDtypeStruct(master.shape, f32), jax.ShapeDtypeStruct((count, width), bf)),
         in_specs=[smem] * 2 + [vmem] * 6 + [anywhere] * 4,
         out_specs=(vmem,) * 2,
         scratch_shapes=[
             pltpu.VMEM(wf.shape, bf),
             pltpu.VMEM(wd.shape, bf),
+            pltpu.VMEM(master.shape, f32),
+            pltpu.VMEM(master.shape, f32),
+            pltpu.VMEM(cube, f32),
             pltpu.VMEM(cube, f32),
             pltpu.VMEM(cube, f32),
             pltpu.VMEM(blocks, bf),
@@ -718,13 +744,13 @@
         ids,
         gains,
         rows,
-        master.reshape(cube),
-        moment.reshape(cube),
-        second.reshape(cube),
+        master,
+        moment,
+        second,
         wf,
         wd,
     )
-    return updated.reshape(master.shape), decoded
+    return updated, decoded
 
 
 def expert_decode(rows, joined_weight, down_weight, flat_bf):

time: 183 us -> 176 us (0.962)
  local copies, waits for them, and re-layouts: 11.5 us -> 6.32 us
  Pallas kernels: 168 us -> 166 us
    reshape x3 -> x0, local copies, waits for them, and re-layouts: 5.09 us -> none  [the longest x1 2.06 us: job(): moment.reshape(cube)]
where the time goes in v3:
time: 176 us; the launch traced here: 175 us
  Pallas kernels  166 us (94%)
  local copies, waits for them, and re-layouts  6.32 us (4%)
  other arithmetic  2.65 us (2%)
    pallas_call x1, Pallas kernels, job(): pl.pallas_call(job_kernel, out_shape=(jax.ShapeDtypeStruct(master.shape,...  166 us
    unnamed x2, local copies, waits for them, and re-layouts  3.55 us

profile of v3, /device:TPU:0, one launch (start us, length us, event | category | flops | bytes accessed | tf_op | source)
XLA Modules:
  0.0 175.4 jit_solution(1664470423868510848)
XLA Ops:
  0.6 1.3 select_reduce_fusion.held_by
  1.9 0.8 copy.19
  2.7 0.7 add_bitcast_fusion
  3.4 0.6 pad.8.ids
  4.0 0.8 copy.20
  4.7 0.7 maximum_bitcast_fusion
  5.4 0.6 pad.9.gains_in
  6.1 165.8 %job.1 = (f32[16,10496]{1,0:T(8,128)}, bf16[32,2048]{1,0:T(8,128)(2,1)}) custom-call(s32[16]{0:T(128)} %owner.1, s32[16]{0:T(128)} %select_reduce_fusion.held_by, bf16[128,2048]{1,0:T(8,128)(2,1)} %tok.1, bf16[128,2048]{1,0:T(8,128)(2,1)} %cot.1, s32[8,256]{1,0:T(8,128)} %pad.8.ids, f32[8,256]{1,0:T(8,128)} %pad.9.gains_in, bf16[32,2048]{1,0:T(8,128)(2,1)} %bitcast.12, ...), custom_call_target="tpu_custom_call" | custom-call | tf_op jit(solution)/shard_map/job/pallas_call | solution.py:681
  171.8 2.0 %copy.23 = f32[16,10496]{1,0:T(8,128)} copy(f32[16,10496]{1,0:T(8,128)} %get-tuple-element.8) | data formatting | bytes 1343488
  173.8 1.6 copy.24
